TPU v7x, 32 devices: a whole 2x2x4 slice. The times are simulated.
32 devices in a mesh: rows: 8 (over z, y), rep: 4 (over x, core).
Axes of the slice: x: 2, y: 2, z: 4, core: 2. Of those that a mesh axis runs over, the one named last changes fastest.
Arguments:
- features: bfloat16 [32768, 512], P('rows', 'rep'), may hold values from -6 to 6
- adjacency: bfloat16 [256, 6, 128, 128], P('rows'), may hold values from -1 to 1
- neighbours: int32 [256, 6], P('rows'), may hold values from 0 to 47, as said below
- occupancy: int32 [256], P('rows'), may hold values from 32 to 128
- send_cells: int32 [8, 8, 2], P('rows'), may hold values from 0 to 31
- weight: bfloat16 [512, 512], replicated, may hold values from -0.25 to 0.25
- cotangent: bfloat16 [32768, 512], P('rows', 'rep'), may hold values from -6 to 6
Outputs:
- output: bfloat16 [32768, 512], P('rows', 'rep')
- weight_grad: float32 [512, 512], P('rep')
- feature_grad: bfloat16 [32768, 512], P('rows', 'rep')
Inputs may be any that keep to these rules, and one draw needn't show every extreme that they name: neighbours[i,0] = i % 32, the cell itself; other entries name any slot.
All inputs are finite; a program needn't handle non-finite values.
Results may differ from a plain program's by a relative error of at most 0.0068.
Values may be sent and summed in bfloat16 or wider, within the bound.
A program may use at most 128 MiB of HBM per device.

v0:
```python
import jax
import jax.numpy as jnp
from jax import lax
from jax.sharding import PartitionSpec as P


def on_device(features, adjacency, neighbours, occupancy, send_cells, weight, cotangent):
    cells, blocks, slots_cell, _ = adjacency.shape
    part = features.shape[1]
    peers = lax.axis_size("rows")
    sending = send_cells.shape[2]
    first = lax.axis_index("rep") * part
    mask = (jnp.arange(slots_cell, dtype=jnp.int32)[None, :] < occupancy[:, None]).astype(
        jnp.float32
    )
    scale = (jnp.sum(jnp.square(adjacency.astype(jnp.float32)), axis=(1, 3)) + 1e-06) ** (-0.25)
    keep = scale * mask
    scaled = (
        features.reshape(cells, slots_cell, part).astype(jnp.float32) * keep[..., None]
    ).astype(jnp.bfloat16)
    outgoing = scaled[send_cells[0]]
    incoming = lax.all_to_all(outgoing, "rows", split_axis=0, concat_axis=0, tiled=True)
    table = jnp.concatenate([scaled, incoming.reshape(peers * sending, slots_cell, part)], axis=0)
    nearby = table[neighbours]
    summed = jnp.einsum("ikrc,ikcf->irf", adjacency, nearby, preferred_element_type=jnp.float32)
    aggregated = (summed * scale[..., None]).astype(jnp.bfloat16).reshape(cells * slots_cell, part)
    w_rows = lax.dynamic_slice_in_dim(weight, first, part, 0)
    partial_terms = jnp.dot(aggregated, w_rows, preferred_element_type=jnp.float32)
    pre = lax.psum_scatter(partial_terms, "rep", scatter_dimension=1, tiled=True)
    mask_rows = mask.reshape(-1)[:, None]
    output = (mask_rows * jax.nn.silu(pre)).astype(jnp.bfloat16)
    sig = jax.nn.sigmoid(pre)
    slope = (cotangent.astype(jnp.float32) * mask_rows * sig * (1.0 + pre * (1.0 - sig))).astype(
        jnp.bfloat16
    )
    piece = lax.all_gather(slope, "rep", axis=1, tiled=True)
    back_sum = lax.dot_general(
        piece, w_rows, (((1,), (1,)), ((), ())), preferred_element_type=jnp.float32
    )
    block_grad = lax.dot_general(
        aggregated, piece, (((0,), (0,)), ((), ())), preferred_element_type=jnp.float32
    )
    grad_rows = block_grad
    back_sum, grad_rows = (back_sum, grad_rows)
    total_rows = cells * slots_cell * peers
    weight_grad = lax.psum(grad_rows, "rows") * float(total_rows) ** (-0.5)
    upstream = (back_sum.reshape(cells, slots_cell, part) * scale[..., None]).astype(jnp.bfloat16)
    contrib = jnp.einsum("ikrc,irf->ikcf", adjacency, upstream, preferred_element_type=jnp.float32)
    table_grad = jax.ops.segment_sum(
        contrib.reshape(cells * blocks, slots_cell, part),
        neighbours.reshape(-1),
        num_segments=cells + peers * sending,
    )
    remote_terms = table_grad[cells:].astype(jnp.bfloat16).reshape(peers, sending, slots_cell, part)
    returned = lax.all_to_all(remote_terms, "rows", split_axis=0, concat_axis=0, tiled=True)
    owned = jax.ops.segment_sum(
        returned.reshape(peers * sending, slots_cell, part).astype(jnp.float32),
        send_cells[0].reshape(-1),
        num_segments=cells,
    )
    gathered = table_grad[:cells] + owned
    feature_grad = (
        (gathered * keep[..., None]).astype(jnp.bfloat16).reshape(cells * slots_cell, part)
    )
    return (output, weight_grad, feature_grad)


def solution(mesh):
    placed = (
        P("rows", "rep"),
        P("rows", None, None, None),
        P("rows", None),
        P("rows"),
        P("rows", None, None),
        P(),
        P("rows", "rep"),
    )
    return jax.shard_map(
        on_device,
        mesh=mesh,
        in_specs=placed,
        out_specs=(P("rows", "rep"), P("rep", None), P("rows", "rep")),
        check_vma=False,
    )
```

profile of v0, /device:TPU:0, one launch (start us, length us, event | category | flops | bytes accessed | tf_op | source)
XLA Modules:
  0.0 334.8 jit_solution(13883536380911547476)
XLA Ops:
  7.2 0.0 copy-start
  7.2 0.0 copy-start.6
  7.2 0.0 copy-start.7
  7.2 0.0 copy-start.4
  7.2 4.2 %multiply_reduce_fusion = f32[32,128]{1,0:T(8,128)S(1)} fusion(bf16[32,6,128,128]{3,2,1,0:T(8,128)(2,1)} %param.8), kind=kLoop, calls=%fused_computation.4 | loop fusion | flops 9433088 | bytes 6307840 | tf_op jit(solution)/shard_map/reduce_sum | solution.py:16
  11.4 0.0 copy-done.6
  11.4 0.1 copy.13
  11.5 0.1 reshape.113
  11.6 0.0 copy-done.7
  11.6 0.1 add_power_fusion
  11.7 0.0 copy-done.4
  11.7 0.0 copy-start.5
  11.7 0.7 fusion
  12.4 1.4 gather_fusion
  13.8 7.3 %all-to-all-start = ((bf16[8,2,128,128]{3,2,1,0:T(8,128)(2,1)}), bf16[8,2,128,128]{3,2,1,0:T(8,128)(2,1)S(1)}, u32[]{:S(2)}, u32[]{:S(2)}) async-start(bf16[8,2,128,128]{3,2,1,0:T(8,128)(2,1)} %bitcast.3), calls=%async_computation | async-start | bytes 1048576 | tf_op jit(solution)/shard_map/all_to_all | solution.py:22
  21.1 0.0 reduce-scatter.2.cloned.1.call-start
  21.1 0.0 copy-done.5
  21.2 0.1 copy.14
  21.2 0.1 reshape.121
  21.4 14.2 %all-to-all-done = bf16[8,2,128,128]{3,2,1,0:T(8,128)(2,1)S(1)} async-done(((bf16[8,2,128,128]{3,2,1,0:T(8,128)(2,1)}), bf16[8,2,128,128]{3,2,1,0:T(8,128)(2,1)S(1)}, u32[]{:S(2)}, u32[]{:S(2)}) %all-to-all-start) | async-done | bytes 524320 | tf_op jit(solution)/shard_map/all_to_all | solution.py:22
  35.6 0.0 copy-start.2
  35.6 0.8 copy-done.2
  36.4 1.2 pad_maximum_fusion
  37.5 8.0 %gather_fusion.1 = bf16[192,128,128]{2,1,0:T(8,128)(2,1)} fusion(bf16[48,128,128]{2,1,0:T(8,128)(2,1)S(1)} %pad_maximum_fusion, s32[1024]{0:T(1024)S(1)} %pad_clamp_fusion), kind=kCustom, calls=%fused_computation.1 | custom fusion | bytes 12583680 | tf_op jit(solution)/shard_map/gather | solution.py:24
  45.6 6.4 %fusion.1 = bf16[32,128,128]{1,2,0:T(8,128)(2,1)S(1)} fusion(bf16[32,6,128,128]{3,2,1,0:T(8,128)(2,1)} %param.8, bf16[32,6,128,128]{3,2,1,0:T(8,128)(2,1)} %bitcast.41, f32[32,128]{1,0:T(8,128)S(1)} %get-tuple-element.5), kind=kOutput, calls=%fused_computation.8 | convolution fusion | flops 806354944 | bytes 13647872 | tf_op jit(solution)/shard_map/ikrc,ikcf->irf/dot_general | solution.py:25
  52.0 0.0 copy-done
  52.0 4.5 %fusion.8 = f32[4096,512]{1,0:T(8,128)} fusion(bf16[4096,128]{1,0:T(8,128)(2,1)S(1)} %bitcast.42, bf16[512,512]{1,0:T(8,128)(2,1)S(1)} %copy-done, s32[]{:T(128)S(6)} %select_n.18), kind=kOutput, calls=%fused_computation.23 | convolution fusion | flops 536870912 | bytes 9568260 | tf_op jit(solution)/shard_map/dot_general | solution.py:28
  56.5 0.0 copy-start.3
  56.5 0.0 reduce-scatter.2.cloned.1.call-update
  56.5 0.2 all-gather.2.cloned.1.call-start
  56.7 0.1 convert_bitcast_fusion
  56.8 70.7 %reduce-scatter.2.cloned.1.call-done = f32[4096,128]{1,0:T(8,128)} async-done(((f32[4096,512]{1,0:T(8,128)}), f32[4096,128]{1,0:T(8,128)}) %reduce-scatter.2.cloned.1.call-update) | async-done | bytes 2097168 | tf_op jit(solution)/shard_map/reduce_scatter | solution.py:29
  127.5 0.0 copy-done.3
  127.5 3.4 %multiply_convert_fusion.2 = (bf16[4096,128]{1,0:T(8,128)(2,1)}, bf16[4096,128]{1,0:T(8,128)(2,1)}) fusion(f32[4096,128]{1,0:T(8,128)} %reduce-scatter.2.cloned.1.call-done, bf16[4096,128]{1,0:T(8,128)(2,1)S(1)} %copy-done.3, f32[4096]{0:T(1024)S(1)} %convert_bitcast_fusion), kind=kLoop, calls=%fused_computation.11 | loop fusion | flops 7340032 | bytes 5259264 | tf_op jit(solution)/shard_map/convert_element_type | solution.py:33
  130.8 0.0 all-gather.2.cloned.1.call-update
  130.9 0.1 copy.15
  131.0 0.1 reshape.129
  131.1 35.0 %all-gather.2.cloned.1.call-done = bf16[4096,512]{1,0:T(8,128)(2,1)} async-done(((bf16[4096,128]{1,0:T(8,128)(2,1)}), bf16[4096,512]{1,0:T(8,128)(2,1)}) %all-gather.2.cloned.1.call-update) | async-done | bytes 4194320 | tf_op jit(solution)/shard_map/all_gather | solution.py:36
  166.0 4.7 %fusion.6 = f32[4096,128]{1,0:T(8,128)} fusion(bf16[4096,512]{1,0:T(8,128)(2,1)} %all-gather.2.cloned.1.call-done, bf16[512,512]{1,0:T(8,128)(2,1)S(1)} %copy-done, s32[]{:T(128)S(6)} %select_n.18), kind=kOutput, calls=%fused_computation.21 | convolution fusion | flops 536870912 | bytes 6422532 | tf_op jit(solution)/shard_map/dot_general | solution.py:37
  170.8 2.9 copy.16
  173.7 9.7 %fusion.3 = f32[32,128,6,128]{3,1,2,0:T(8,128)} fusion(bf16[32,6,128,128]{3,2,1,0:T(8,128)(2,1)} %param.8, f32[32,128,128]{1,2,0:T(8,128)} %copy.16, f32[32,128]{1,0:T(8,128)S(1)} %get-tuple-element.5), kind=kOutput, calls=%fused_computation.16 | convolution fusion | flops 806354944 | bytes 20987904 | tf_op jit(solution)/shard_map/ikrc,irf->ikcf/dot_general | solution.py:48
  183.4 12.6 %copy.17 = f32[192,128,128]{2,1,0:T(8,128)} copy(f32[192,128,128]{1,2,0:T(8,128)} %bitcast.40) | data formatting | bytes 25165824 | tf_op jit(solution)/shard_map/reshape | solution.py:50
  196.0 2.0 broadcast_in_dim.5
  198.0 39.6 %scatter_fusion = f32[48,128,128]{2,1,0:T(8,128)} fusion(f32[48,128,128]{2,1,0:T(8,128)} %broadcast_in_dim.5, s32[192]{0:T(256)S(1)} %reshape.129, f32[192,128,128]{2,1,0:T(8,128)} %copy.17), kind=kCustom, calls=%fused_computation.2 | custom fusion | flops 3145728 | bytes 37749504 | tf_op jit(solution)/shard_map/scatter-add | solution.py:49
  237.6 2.1 slice.16
  239.7 5.5 %all-to-all-start.1 = ((bf16[8,2,128,128]{3,2,1,0:T(8,128)(2,1)}), bf16[8,2,128,128]{3,2,1,0:T(8,128)(2,1)S(1)}, u32[]{:S(2)}, u32[]{:S(2)}) async-start(bf16[8,2,128,128]{3,2,1,0:T(8,128)(2,1)} %bitcast.16), calls=%async_computation.2 | async-start | bytes 1048576 | tf_op jit(solution)/shard_map/all_to_all | solution.py:55
  245.2 0.0 all-reduce.2.cloned.1.call-start
  245.2 3.6 %fusion.13 = f32[128,512]{1,0:T(8,128)} fusion(bf16[4096,128]{1,0:T(8,128)(2,1)S(1)} %bitcast.43, bf16[4096,512]{1,0:T(8,128)(2,1)} %all-gather.2.cloned.1.call-done), kind=kOutput, calls=%fused_computation.35 | convolution fusion | flops 536870912 | bytes 5505024 | tf_op jit(solution)/shard_map/dot_general | solution.py:40
  248.9 0.0 all-reduce.2.cloned.1.call-update
  248.9 0.1 copy.18
  249.0 0.1 reshape.137
  249.1 1.7 slice.13
  250.8 70.6 %all-reduce.2.cloned.1.call-done = f32[128,512]{1,0:T(8,128)} async-done(((f32[128,512]{1,0:T(8,128)}), f32[128,512]{1,0:T(8,128)}) %all-reduce.2.cloned.1.call-update) | async-done | bytes 262160 | tf_op jit(solution)/shard_map/psum | solution.py:46
  321.4 1.7 broadcast_multiply_fusion
  323.1 0.0 all-to-all-done.1
  323.1 1.1 bitcast_convert_fusion
  324.2 0.0 copy-start.1
  324.2 2.6 scatter_fusion.1
  326.8 1.5 multiply_convert_fusion
  328.3 0.0 copy-done.1
  (4 shorter events, 0.0 us)
Async XLA Ops:
  7.2 44.8 %copy-start = (bf16[512,512]{1,0:T(8,128)(2,1)S(1)}, bf16[512,512]{1,0:T(8,128)(2,1)}, u32[]{:S(2)}) copy-start(bf16[512,512]{1,0:T(8,128)(2,1)} %param.12) | copy-start | bytes 1572868
  7.2 4.2 %copy-start.6 = (s32[1,8,2]{1,2,0:T(2,128)S(1)}, s32[1,8,2]{1,2,0:T(2,128)}, u32[]{:S(2)}) copy-start(s32[1,8,2]{1,2,0:T(2,128)} %param.11) | copy-start | bytes 196
  7.2 4.4 %copy-start.7 = (s32[32]{0:T(128)S(1)}, s32[32]{0:T(128)}, u32[]{:S(2)}) copy-start(s32[32]{0:T(128)} %param.10) | copy-start | bytes 388
  7.2 4.5 %copy-start.4 = (bf16[4096,128]{1,0:T(8,128)(2,1)S(1)}, bf16[4096,128]{1,0:T(8,128)(2,1)}, u32[]{:S(2)}) copy-start(bf16[4096,128]{1,0:T(8,128)(2,1)} %param.7) | copy-start | bytes 3145732
  11.7 9.4 %copy-start.5 = (s32[32,6]{0,1:T(8,128)S(1)}, s32[32,6]{0,1:T(8,128)}, u32[]{:S(2)}) copy-start(s32[32,6]{0,1:T(8,128)} %param.9) | copy-start | bytes 2308
  13.8 21.8 %all-to-all-start = ((bf16[8,2,128,128]{3,2,1,0:T(8,128)(2,1)}), bf16[8,2,128,128]{3,2,1,0:T(8,128)(2,1)S(1)}, u32[]{:S(2)}, u32[]{:S(2)}) async-start(bf16[8,2,128,128]{3,2,1,0:T(8,128)(2,1)} %bitcast.3), calls=%async_computation | async-start | bytes 1048576 | tf_op jit(solution)/shard_map/all_to_all | solution.py:22
  21.1 106.4 %reduce-scatter.2.cloned.1.call-start = ((), (), s32[]{:S(2)}) async-start(), calls=%async_computation.3 | async-start | bytes 10485760 | tf_op jit(solution)/shard_map/reduce_scatter | solution.py:29
  35.6 0.8 copy-start.2
  56.5 71.0 %copy-start.3 = (bf16[4096,128]{1,0:T(8,128)(2,1)S(1)}, bf16[4096,128]{1,0:T(8,128)(2,1)}, u32[]{:S(2)}) copy-start(bf16[4096,128]{1,0:T(8,128)(2,1)} %param.13) | copy-start | bytes 3145732
  56.5 109.5 %all-gather.2.cloned.1.call-start = ((), (), s32[]{:S(2)}) async-start(), calls=%async_computation.4 | async-start | bytes 5242880 | tf_op jit(solution)/shard_map/all_gather | solution.py:36
  239.7 83.4 %all-to-all-start.1 = ((bf16[8,2,128,128]{3,2,1,0:T(8,128)(2,1)}), bf16[8,2,128,128]{3,2,1,0:T(8,128)(2,1)S(1)}, u32[]{:S(2)}, u32[]{:S(2)}) async-start(bf16[8,2,128,128]{3,2,1,0:T(8,128)(2,1)} %bitcast.16), calls=%async_computation.2 | async-start | bytes 1048576 | tf_op jit(solution)/shard_map/all_to_all | solution.py:55
  245.2 76.2 %all-reduce.2.cloned.1.call-start = ((), (), s32[]{:S(2)}) async-start(), calls=%async_computation.5 | async-start | bytes 524288 | tf_op jit(solution)/shard_map/psum | solution.py:46
  324.2 4.1 %copy-start.1 = (bf16[512,512]{1,0:T(8,128)(2,1)S(1)}, bf16[512,512]{1,0:T(8,128)(2,1)}, u32[]{:S(2)}) copy-start(bf16[512,512]{1,0:T(8,128)(2,1)} %param.12) | copy-start | bytes 1572868
Sparse Core Ops, SparseCore 0:
  56.6 70.7 reduce-scatter.1
  131.0 35.0 all-gather.1
  250.3 71.0 all-reduce.1
where the time goes:
time: 336 us; the launch traced here: 335 us
  waiting for transfers between devices  190 us (57%)
  other arithmetic  56.1 us (17%)
  local copies, waits for them, and re-layouts  32.4 us (10%)
  matrix products  28.9 us (9%)
  between operations  13.9 us (4%)
  starting transfers between devices  13.1 us (4%)
    reduce_scatter x1, waiting for transfers between devices, on_device(): lax.psum_scatter(partial_terms, 'rep', scatter_dimension=1, tiled=True)  70.7 us
    psum x1, waiting for transfers between devices, on_device(): weight_grad = lax.psum(grad_rows, 'rows') * float(total_rows) ** (-0.5)  70.6 us
    scatter-add x1, other arithmetic, on_device(): jax.ops.segment_sum(contrib.reshape(cells * blocks, slots_cell, part), ne...  39.6 us
    all_gather x1, waiting for transfers between devices, on_device(): piece = lax.all_gather(slope, 'rep', axis=1, tiled=True)  35 us
    all_to_all x1, waiting for transfers between devices, on_device(): lax.all_to_all(outgoing, 'rows', split_axis=0, concat_axis=0, tiled=True)  14.2 us
    reshape x1, local copies, waits for them, and re-layouts, on_device(): contrib.reshape(cells * blocks, slots_cell, part)  12.6 us
    dot_general x1, matrix products, on_device(): jnp.einsum('ikrc,irf->ikcf', adjacency, upstream, preferred_element_type=...  9.69 us
    gather x1, local copies, waits for them, and re-layouts, on_device(): nearby = table[neighbours]  8.05 us
  transfers between devices with their start and end apart: 5, of which 4 were waited for; matrix products, arithmetic and copies ran while one was open for 2% of the time, Pallas kernels for 0%

commit v1 on v0

v1 whole, which is shorter than its diff:
```python
import functools

import jax
import jax.numpy as jnp
from jax import lax
from jax.experimental import pallas as pl
from jax.experimental.pallas import tpu as pltpu
from jax.sharding import PartitionSpec as P

MESH = pl.DeviceIdType.MESH
F32 = jnp.float32
BF16 = jnp.bfloat16
SMEM = pltpu.SMEM
VMEM = pltpu.VMEM


def params(**kw):
    return pltpu.CompilerParams(vmem_limit_bytes=56 * 1024 * 1024, **kw)


def whole_block(shape):
    return pl.BlockSpec(shape, lambda *_: (0,) * len(shape))


def row_mask(count, slots):
    rows = lax.broadcasted_iota(jnp.int32, (slots, 1), 0)
    return jnp.where(rows < count, 1.0, 0.0).astype(F32)


def prepare_body(step_cells, occ, send, feat, adj, scale_out, scaled_out, outgoing):
    step = pl.program_id(0)
    slots = adj.shape[2]
    for j in range(step_cells):
        cell = step * step_cells + j
        total = jnp.zeros((slots, slots), F32)
        for k in range(adj.shape[1]):
            a = adj[j, k].astype(F32)
            total += a * a
        s = jnp.sum(total, axis=1, keepdims=True) + 1e-6
        scale = lax.rsqrt(jnp.sqrt(s))
        scale_out[j] = jnp.broadcast_to(scale, scale_out.shape[1:])
        keep = scale * row_mask(occ[cell], slots)
        scaled_out[cell] = (feat[j].astype(F32) * keep).astype(BF16)

    @pl.when(step == pl.num_programs(0) - 1)
    def _():
        def put(t, carry):
            outgoing[t] = scaled_out[send[t]]
            return carry

        lax.fori_loop(0, outgoing.shape[0], put, 0)


def prepare(features, adjacency, occupancy, send):
    cells, blocks, slots, _ = adjacency.shape
    part = features.shape[2]
    n = 4
    count = send.shape[0]
    return pl.pallas_call(
        functools.partial(prepare_body, n),
        grid=(cells // n,),
        in_specs=[
            pl.BlockSpec(memory_space=SMEM),
            pl.BlockSpec(memory_space=SMEM),
            pl.BlockSpec((n, slots, part), lambda i: (i, 0, 0)),
            pl.BlockSpec((n, blocks, slots, slots), lambda i: (i, 0, 0, 0)),
        ],
        out_specs=[
            pl.BlockSpec((n, slots, part), lambda i: (i, 0, 0)),
            whole_block((cells, slots, part)),
            whole_block((count, slots, part)),
        ],
        out_shape=[
            jax.ShapeDtypeStruct((cells, slots, part), F32),
            jax.ShapeDtypeStruct((cells, slots, part), BF16),
            jax.ShapeDtypeStruct((count, slots, part), BF16),
        ],
        compiler_params=params(),
        name="prepare",
    )(occupancy, send, features, adjacency)


def aggregate_body(step_cells, neigh, scaled, incoming, scale, adj, out, table):
    step = pl.program_id(0)
    blocks = adj.shape[1]
    cells = scaled.shape[0]

    @pl.when(step == 0)
    def _():
        table[pl.ds(0, cells)] = scaled[...]
        table[pl.ds(cells, incoming.shape[0])] = incoming[...]

    for j in range(step_cells):
        cell = step * step_cells + j
        near = jnp.concatenate([table[neigh[cell * blocks + k]] for k in range(blocks)], axis=0)
        wide = jnp.concatenate([adj[j, k] for k in range(blocks)], axis=1)
        total = jnp.dot(wide, near, preferred_element_type=F32)
        out[j] = (total * scale[j]).astype(BF16)


def aggregate(neigh, scaled, incoming, scale, adjacency):
    cells, blocks, slots, _ = adjacency.shape
    part = scaled.shape[2]
    n = 4
    return pl.pallas_call(
        functools.partial(aggregate_body, n),
        grid=(cells // n,),
        in_specs=[
            pl.BlockSpec(memory_space=SMEM),
            whole_block(scaled.shape),
            whole_block(incoming.shape),
            pl.BlockSpec((n, slots, part), lambda i: (i, 0, 0)),
            pl.BlockSpec((n, blocks, slots, slots), lambda i: (i, 0, 0, 0)),
        ],
        out_specs=pl.BlockSpec((n, slots, part), lambda i: (i, 0, 0)),
        out_shape=jax.ShapeDtypeStruct((cells, slots, part), BF16),
        scratch_shapes=[VMEM((cells + incoming.shape[0], slots, part), BF16)],
        compiler_params=params(),
        name="aggregate",
    )(neigh, scaled, incoming, scale, adjacency)


def middle_body(step_cells, first, occ, agg, cot, scale, weight, out, up, wgrad, acc):
    step = pl.program_id(0)
    reps, rows, part = agg.shape
    slots = rows // step_cells
    base = first[0] + step * step_cells
    a = jnp.concatenate([agg[q] for q in range(reps)], axis=1)
    pre = jnp.dot(a, weight[...], preferred_element_type=F32)
    mask = jnp.concatenate([row_mask(occ[base + j], slots) for j in range(step_cells)], axis=0)
    sig = 0.5 * jnp.tanh(0.5 * pre) + 0.5
    o = (mask * (pre * sig)).astype(BF16)
    c = jnp.concatenate([cot[q] for q in range(reps)], axis=1).astype(F32)
    slope = (c * mask * sig * (1.0 + pre * (1.0 - sig))).astype(BF16)
    back = lax.dot_general(slope, weight[...], (((1,), (1,)), ((), ())), preferred_element_type=F32)
    s = scale[...].reshape(rows, part)
    for q in range(reps):
        cols = slice(q * part, (q + 1) * part)
        out[q] = o[:, cols]
        up[q] = (back[:, cols] * s).astype(BF16)
    term = lax.dot_general(a, slope, (((0,), (0,)), ((), ())), preferred_element_type=F32)

    @pl.when(step == 0)
    def _():
        acc[...] = term

    @pl.when(step > 0)
    def _():
        acc[...] += term

    @pl.when(step == pl.num_programs(0) - 1)
    def _():
        wgrad[...] = acc[...].astype(BF16)


def middle(first, occupancy, agg, cot, scale, weight):
    reps, rows, part = agg.shape
    slots = scale.shape[1]
    n = 2
    step_rows = n * slots
    width = weight.shape[1]
    row_block = pl.BlockSpec((reps, step_rows, part), lambda i, f: (0, i, 0))
    return pl.pallas_call(
        functools.partial(middle_body, n),
        grid_spec=pltpu.PrefetchScalarGridSpec(
            num_scalar_prefetch=1,
            grid=(rows // step_rows,),
            in_specs=[
                pl.BlockSpec(memory_space=SMEM),
                row_block,
                row_block,
                pl.BlockSpec((n, slots, part), lambda i, f: (f[0] // n + i, 0, 0)),
                whole_block(weight.shape),
            ],
            out_specs=[row_block, row_block, whole_block(weight.shape)],
            scratch_shapes=[VMEM((reps * part, width), F32)],
        ),
        out_shape=[
            jax.ShapeDtypeStruct((reps, rows, part), BF16),
            jax.ShapeDtypeStruct((reps, rows, part), BF16),
            jax.ShapeDtypeStruct(weight.shape, BF16),
        ],
        compiler_params=params(),
        name="middle",
    )(first, occupancy, agg, cot, scale, weight)


def spread_body(step_cells, neigh, up, adj, local, remote, table):
    step = pl.program_id(0)
    blocks, slots = adj.shape[1], adj.shape[2]

    @pl.when(step == 0)
    def _():
        table[...] = jnp.zeros_like(table)

    for j in range(step_cells):
        cell = step * step_cells + j
        wide = jnp.concatenate([adj[j, k] for k in range(blocks)], axis=1)
        terms = lax.dot_general(wide, up[j], (((0,), (0,)), ((), ())), preferred_element_type=F32)
        for k in range(blocks):
            slot = neigh[cell * blocks + k]
            table[slot] = table[slot] + terms[k * slots : (k + 1) * slots]

    @pl.when(step == pl.num_programs(0) - 1)
    def _():
        cells = local.shape[0]
        local[...] = table[pl.ds(0, cells)]
        remote[...] = table[pl.ds(cells, remote.shape[0])].astype(BF16)


def spread(neigh, up, adjacency, received):
    cells, blocks, slots, _ = adjacency.shape
    part = up.shape[2]
    n = 4
    return pl.pallas_call(
        functools.partial(spread_body, n),
        grid=(cells // n,),
        in_specs=[
            pl.BlockSpec(memory_space=SMEM),
            pl.BlockSpec((n, slots, part), lambda i: (i, 0, 0)),
            pl.BlockSpec((n, blocks, slots, slots), lambda i: (i, 0, 0, 0)),
        ],
        out_specs=[whole_block((cells, slots, part)), whole_block((received, slots, part))],
        out_shape=[
            jax.ShapeDtypeStruct((cells, slots, part), F32),
            jax.ShapeDtypeStruct((received, slots, part), BF16),
        ],
        scratch_shapes=[VMEM((cells + received, slots, part), F32)],
        compiler_params=params(),
        name="spread",
    )(neigh, up, adjacency)


def combine_body(send, occ, local, returned, scale, out, total):
    slots = local.shape[1]
    total[...] = local[...]

    def add(t, carry):
        cell = send[t]
        total[cell] = total[cell] + returned[t].astype(F32)
        return carry

    lax.fori_loop(0, returned.shape[0], add, 0)

    def finish(i, carry):
        out[i] = (total[i] * (scale[i] * row_mask(occ[i], slots))).astype(BF16)
        return carry

    lax.fori_loop(0, local.shape[0], finish, 0)


def combine(send, occupancy, local, returned, scale):
    return pl.pallas_call(
        combine_body,
        in_specs=[pl.BlockSpec(memory_space=SMEM)] * 2 + [pl.BlockSpec(memory_space=VMEM)] * 3,
        out_specs=pl.BlockSpec(memory_space=VMEM),
        out_shape=jax.ShapeDtypeStruct(local.shape, BF16),
        scratch_shapes=[VMEM(local.shape, F32)],
        compiler_params=params(),
        name="combine",
    )(send, occupancy, local, returned, scale)


def greet(axes):
    barrier = pltpu.get_barrier_semaphore()
    expected = 0
    for axis in axes:
        size = lax.axis_size(axis)
        me = lax.axis_index(axis)
        for d in range(1, size):
            pl.semaphore_signal(
                barrier, inc=1, device_id={axis: lax.rem(me + d, size)}, device_id_type=MESH
            )
        expected += size - 1
    pl.semaphore_wait(barrier, expected)


def start_exchange(axis, src, dst, sends, recvs, own):
    size = lax.axis_size(axis)
    me = lax.axis_index(axis)
    copies = []
    for d in range(1, size):
        peer = lax.rem(me + d, size)
        copy = pltpu.make_async_remote_copy(
            src_ref=src.at[peer],
            dst_ref=dst.at[me],
            send_sem=sends.at[d],
            recv_sem=recvs.at[d],
            device_id={axis: peer},
            device_id_type=MESH,
        )
        copy.start()
        copies.append(copy)
    mine = pltpu.make_async_copy(src.at[me], dst.at[me], own)
    mine.start()
    copies.append(mine)
    return copies


def exchange_body(axes, *refs):
    n = len(axes)
    srcs, dsts, sems = refs[:n], refs[n : 2 * n], refs[2 * n :]
    greet(sorted(set(axes)))
    copies = []
    for i, axis in enumerate(axes):
        copies += start_exchange(axis, srcs[i], dsts[i], sems[3 * i], sems[3 * i + 1], sems[3 * i + 2])
    for copy in copies:
        copy.wait()


def exchange_sems(axes):
    sems = []
    for axis in axes:
        size = lax.axis_size(axis)
        sems += [
            pltpu.SemaphoreType.DMA((size,)),
            pltpu.SemaphoreType.DMA((size,)),
            pltpu.SemaphoreType.DMA,
        ]
    return sems


def exchange(axes, arrays, collective_id, name):
    return pl.pallas_call(
        functools.partial(exchange_body, axes),
        in_specs=[pl.BlockSpec(memory_space=pl.ANY)] * len(arrays),
        out_specs=[pl.BlockSpec(memory_space=pl.ANY)] * len(arrays),
        out_shape=[jax.ShapeDtypeStruct(a.shape, a.dtype) for a in arrays],
        scratch_shapes=exchange_sems(axes),
        compiler_params=params(collective_id=collective_id, has_side_effects=True),
        name=name,
    )(*arrays)


def last_body(factor, terms, out_rows, wgrad, returned, out, grad, ph1, held, ph2, *sems):
    greet(("rep", "rows"))
    first = start_exchange("rep", wgrad, ph1, *sems[0:3])
    others = start_exchange("rows", terms, returned, *sems[3:6])
    others += start_exchange("rep", out_rows, out, *sems[6:9])
    for copy in first:
        copy.wait()
    total = ph1[0].astype(F32)
    for q in range(1, ph1.shape[0]):
        total += ph1[q].astype(F32)
    peers = lax.axis_size("rows")
    if ph2 is None:
        grad[...] = total
    else:
        held[...] = total.astype(BF16).reshape(held.shape)
        for copy in start_exchange("rows", held, ph2, *sems[9:12]):
            copy.wait()
        total = ph2[0].astype(F32)
        for p in range(1, peers):
            total += ph2[p].astype(F32)
        me = lax.axis_index("rows")
        grad[me] = total * factor
        copies = []
        for d in range(1, peers):
            copy = pltpu.make_async_remote_copy(
                src_ref=grad.at[me],
                dst_ref=grad.at[me],
                send_sem=sems[12].at[d],
                recv_sem=sems[13].at[d],
                device_id={"rows": lax.rem(me + d, peers)},
                device_id_type=MESH,
            )
            copy.start()
            copies.append(copy)
        for copy in copies:
            copy.wait()
    for copy in others:
        copy.wait()


def last_exchange(terms, out_rows, wgrad, factor, collective_id):
    peers = lax.axis_size("rows")
    reps, part, width = wgrad.shape
    cut = part % (16 * peers) == 0
    axes = ("rep", "rows", "rep", "rows")
    scratch = [VMEM(wgrad.shape, BF16)]
    if cut:
        scratch += [VMEM((peers, part // peers, width), BF16)] * 2
        grad_shape = (peers, part // peers, width)
        scratch += exchange_sems(axes)
        scratch += [pltpu.SemaphoreType.DMA((peers,))] * 2
        body = functools.partial(last_body, factor)
    else:
        grad_shape = (part, width)
        scratch += exchange_sems(axes[:3])

        def body(t, o, w, r, out, grad, ph1, *sems):
            last_body(factor, t, o, w, r, out, grad, ph1, None, None, *sems)

    returned, out, grad = pl.pallas_call(
        body,
        in_specs=[pl.BlockSpec(memory_space=pl.ANY)] * 3,
        out_specs=[pl.BlockSpec(memory_space=pl.ANY)] * 2 + [pl.BlockSpec(memory_space=VMEM)],
        out_shape=[
            jax.ShapeDtypeStruct(terms.shape, BF16),
            jax.ShapeDtypeStruct(out_rows.shape, BF16),
            jax.ShapeDtypeStruct(grad_shape, F32),
        ],
        scratch_shapes=scratch,
        compiler_params=params(collective_id=collective_id, has_side_effects=True),
        name="last_exchange",
    )(terms, out_rows, wgrad)
    if not cut:
        grad = lax.psum(grad, "rows") * factor
    return returned, out, grad.reshape(part, width)


def on_device(features, adjacency, neighbours, occupancy, send_cells, weight, cotangent):
    cells, blocks, slots, _ = adjacency.shape
    part = features.shape[1]
    peers, reps = lax.axis_size("rows"), lax.axis_size("rep")
    sending = send_cells.shape[2]
    rows = cells * slots
    share = rows // reps
    send = send_cells.reshape(-1)
    neigh = neighbours.reshape(-1)
    table = (peers, sending * slots, part)
    cell_shape = (cells, slots, part)

    scale, scaled, outgoing = prepare(features.reshape(cell_shape), adjacency, occupancy, send)
    incoming, cot = exchange(
        ("rows", "rep"),
        (outgoing.reshape(table), cotangent.reshape(reps, share, part)),
        1,
        "first_exchange",
    )
    agg = aggregate(neigh, scaled, incoming.reshape(-1, slots, part), scale, adjacency)
    (agg_rows,) = exchange(("rep",), (agg.reshape(reps, share, part),), 2, "to_rows")
    first = (lax.axis_index("rep") * (cells // reps)).astype(jnp.int32).reshape(1)
    out_rows, up_rows, wgrad = middle(first, occupancy, agg_rows, cot, scale, weight)
    (up,) = exchange(("rep",), (up_rows,), 3, "to_columns")
    local, remote = spread(neigh, up.reshape(cell_shape), adjacency, peers * sending)
    factor = float(rows * peers) ** (-0.5)
    returned, output, weight_grad = last_exchange(
        remote.reshape(table), out_rows, wgrad.reshape(reps, part, -1), factor, 4
    )
    feature_grad = combine(send, occupancy, local, returned.reshape(-1, slots, part), scale)
    return output.reshape(rows, part), weight_grad, feature_grad.reshape(rows, part)


def solution(mesh):
    placed = (
        P("rows", "rep"),
        P("rows", None, None, None),
        P("rows", None),
        P("rows"),
        P("rows", None, None),
        P(),
        P("rows", "rep"),
    )
    return jax.shard_map(
        on_device,
        mesh=mesh,
        in_specs=placed,
        out_specs=(P("rows", "rep"), P("rep", None), P("rows", "rep")),
        check_vma=False,
    )
```

time: 336 us -> 116 us (0.35)
  waiting for transfers between devices: 190 us -> 0 us
  Pallas kernels: 0 us -> 110 us
  other arithmetic: 56.1 us -> 0 us
  matrix products: 28.9 us -> 0 us
  local copies, waits for them, and re-layouts: 32.4 us -> 4.65 us
  between operations: 13.9 us -> 0.68 us
  starting transfers between devices: 13.1 us -> 0 us
    pallas_call x0 -> x9, Pallas kernels: none -> 110 us  [the longest x3 45.9 us: exchange(): pl.pallas_call(functools.partial(exchange_body, axes), in_specs=[pl.Block...]
    reduce_scatter x1 -> x0, waiting for transfers between devices: 70.7 us -> none  [on_device(): lax.psum_scatter(partial_terms, 'rep', scatter_dimension=1, tiled=True)]
    psum x1 -> x0, waiting for transfers between devices: 70.6 us -> none  [on_device(): weight_grad = lax.psum(grad_rows, 'rows') * float(total_rows) ** (-0.5)]
    scatter-add x2 -> x0, other arithmetic: 42.2 us -> none  [the longest x1 39.6 us: on_device(): jax.ops.segment_sum(contrib.reshape(cells * blocks, slots_cell, part), ne...]
    all_gather x1 -> x0, waiting for transfers between devices: 35 us -> none  [on_device(): piece = lax.all_gather(slope, 'rep', axis=1, tiled=True)]
    dot_general x5 -> x0, matrix products: 28.9 us -> none  [the longest x1 9.69 us: on_device(): jnp.einsum('ikrc,irf->ikcf', adjacency, upstream, preferred_element_type=...]
    all_to_all x2 -> x0, waiting for transfers between devices: 14.2 us -> none  [the longest x1 14.2 us: on_device(): lax.all_to_all(outgoing, 'rows', split_axis=0, concat_axis=0, tiled=True)]
    reshape x2, local copies, waits for them, and re-layouts: 15.5 us -> 1.33 us  [the longest x1 0.67 us: on_device(): neigh = neighbours.reshape(-1)]
  transfers between devices with their start and end apart: 5 -> 0, of which waited for: 4 -> 0; matrix products, arithmetic and copies ran while one was open for 2% -> 0% of each run, Pallas kernels for 0% -> 0%
where the time goes in v1:
time: 116 us; the launch traced here: 115 us
  Pallas kernels  110 us (95%)
  local copies, waits for them, and re-layouts  4.65 us (4%)
    pallas_call x3, Pallas kernels, exchange(): pl.pallas_call(functools.partial(exchange_body, axes), in_specs=[pl.Block...  45.9 us
    pallas_call x1, Pallas kernels, last_exchange(): pl.pallas_call(body, in_specs=[pl.BlockSpec(memory_space=pl.ANY)] * 3, ou...  27.1 us
    pallas_call x1, Pallas kernels, spread(): pl.pallas_call(functools.partial(spread_body, n), grid=(cells // n,), in_...  9.18 us
    pallas_call x1, Pallas kernels, aggregate(): pl.pallas_call(functools.partial(aggregate_body, n), grid=(cells // n,),...  8.66 us
    pallas_call x1, Pallas kernels, prepare(): pl.pallas_call(functools.partial(prepare_body, n), grid=(cells // n,), in...  8.18 us
    pallas_call x1, Pallas kernels, middle(): pl.pallas_call(functools.partial(middle_body, n), grid_spec=pltpu.Prefetc...  6.45 us
    pallas_call x1, Pallas kernels, combine(): pl.pallas_call(combine_body, in_specs=[pl.BlockSpec(memory_space=SMEM)] *...  4.31 us
    unnamed x8, local copies, waits for them, and re-layouts  3.32 us

profile of v1, /device:TPU:0, one launch (start us, length us, event | category | flops | bytes accessed | tf_op | source)
XLA Modules:
  0.0 115.1 jit_solution(15969171329619511562)
XLA Ops:
  0.6 0.8 copy.12
  1.4 0.7 reshape.53.send
  2.1 0.8 copy.11
  2.8 0.7 reshape.51.neigh
  3.5 8.2 %prepare.1 = (f32[32,128,128]{2,1,0:T(8,128)}, bf16[32,128,128]{2,1,0:T(8,128)(2,1)}, bf16[16,128,128]{2,1,0:T(8,128)(2,1)}) custom-call(s32[32]{0:T(128)} %occ.5, s32[16]{0:T(128)} %reshape.53.send, bf16[32,128,128]{2,1,0:T(8,128)(2,1)} %bitcast.17, bf16[32,6,128,128]{3,2,1,0:T(8,128)(2,1)} %adj.5), custom_call_target="tpu_custom_call" | custom-call | tf_op jit(solution)/shard_map/prepare/pallas_call | solution.py:59
  11.7 17.8 %first_exchange.1 = (bf16[8,256,128]{2,1,0:T(8,128)(2,1)}, bf16[4,1024,128]{2,1,0:T(8,128)(2,1)}) custom-call(bf16[8,256,128]{2,1,0:T(8,128)(2,1)} %bitcast.20, bf16[4,1024,128]{2,1,0:T(8,128)(2,1)} %bitcast.15), custom_call_target="tpu_custom_call" | custom-call | tf_op jit(solution)/shard_map/first_exchange/pallas_call | solution.py:324
  29.4 8.7 %aggregate.1 = bf16[32,128,128]{2,1,0:T(8,128)(2,1)} custom-call(s32[192]{0:T(256)} %reshape.51.neigh, bf16[32,128,128]{2,1,0:T(8,128)(2,1)} %get-tuple-element.16.scaled, bf16[16,128,128]{2,1,0:T(8,128)(2,1)} %bitcast.21, f32[32,128,128]{2,1,0:T(8,128)} %get-tuple-element.19.scale, bf16[32,6,128,128]{3,2,1,0:T(8,128)(2,1)} %adj.5), custom_call_target="tpu_custom_call" | custom-call | tf_op jit(solution)/shard_map/aggregate/pallas_call | solution.py:105
  38.1 14.1 %to_rows.1.agg = bf16[4,1024,128]{2,1,0:T(8,128)(2,1)} custom-call(bf16[4,1024,128]{2,1,0:T(8,128)(2,1)} %bitcast.14), custom_call_target="tpu_custom_call" | custom-call | tf_op jit(solution)/shard_map/to_rows/pallas_call | solution.py:324
  52.2 6.4 %middle.1 = (bf16[4,1024,128]{2,1,0:T(8,128)(2,1)}, bf16[4,1024,128]{2,1,0:T(8,128)(2,1)}, bf16[512,512]{1,0:T(8,128)(2,1)}) custom-call(s32[1]{0:T(128)} %bitcast.first, s32[32]{0:T(128)} %occ.5, bf16[4,1024,128]{2,1,0:T(8,128)(2,1)} %to_rows.1.agg, bf16[4,1024,128]{2,1,0:T(8,128)(2,1)} %get-tuple-element.20.cot, f32[32,128,128]{2,1,0:T(8,128)} %get-tuple-element.19.scale, ...), custom_call_target="tpu_custom_call" | custom-call | tf_op jit(solution)/shard_map/middle/pallas_call | solution.py:163
  58.6 14.1 %to_columns.1 = bf16[4,1024,128]{2,1,0:T(8,128)(2,1)} custom-call(bf16[4,1024,128]{2,1,0:T(8,128)(2,1)} %get-tuple-element.21.refs_0_), custom_call_target="tpu_custom_call" | custom-call | tf_op jit(solution)/shard_map/to_columns/pallas_call | solution.py:324
  72.7 9.2 %spread.1 = (f32[32,128,128]{2,1,0:T(8,128)}, bf16[16,128,128]{2,1,0:T(8,128)(2,1)}) custom-call(s32[192]{0:T(256)} %reshape.51.neigh, bf16[32,128,128]{2,1,0:T(8,128)(2,1)} %bitcast.13, bf16[32,6,128,128]{3,2,1,0:T(8,128)(2,1)} %adj.5), custom_call_target="tpu_custom_call" | custom-call | tf_op jit(solution)/shard_map/spread/pallas_call | solution.py:215
  81.9 27.1 %last_exchange.1 = (bf16[8,256,128]{2,1,0:T(8,128)(2,1)}, bf16[4,1024,128]{2,1,0:T(8,128)(2,1)}, f32[8,16,512]{2,1,0:T(8,128)}) custom-call(bf16[8,256,128]{2,1,0:T(8,128)(2,1)} %bitcast.23, bf16[4,1024,128]{2,1,0:T(8,128)(2,1)} %get-tuple-element.23.out_rows, bf16[4,128,512]{2,1,0:T(8,128)(2,1)} %bitcast.22), custom_call_target="tpu_custom_call" | custom-call | tf_op jit(solution)/shard_map/last_exchange/pallas_call | solution.py:394
  109.0 0.0 copy-start
  109.0 4.3 %combine.1 = bf16[32,128,128]{2,1,0:T(8,128)(2,1)} custom-call(s32[16]{0:T(128)} %reshape.53.send, s32[32]{0:T(128)} %occ.5, f32[32,128,128]{2,1,0:T(8,128)} %get-tuple-element.27.local, bf16[16,128,128]{2,1,0:T(8,128)(2,1)} %bitcast.19, f32[32,128,128]{2,1,0:T(8,128)} %get-tuple-element.19.scale), custom_call_target="tpu_custom_call" | custom-call | tf_op jit(solution)/shard_map/combine/pallas_call | solution.py:253
  113.3 0.0 copy-start.1
  113.3 0.0 copy-done
  113.3 1.0 copy.15
  114.3 0.1 copy-done.1
  114.4 0.7 copy.16
Async XLA Ops:
  109.0 4.3 %copy-start = (bf16[4,1024,128]{2,1,0:T(8,128)(2,1)S(1)}, bf16[4,1024,128]{2,1,0:T(8,128)(2,1)}, u32[]{:S(2)}) copy-start(bf16[4,1024,128]{2,1,0:T(8,128)(2,1)} %get-tuple-element.25) | copy-start | bytes 3145732
  113.3 1.1 copy-start.1

commit v2 on v0

v2 whole, which is shorter than its diff:
```python
import functools

import jax
import jax.numpy as jnp
from jax import lax
from jax.experimental import pallas as pl
from jax.experimental.pallas import tpu as pltpu
from jax.sharding import PartitionSpec as P

MESH = pl.DeviceIdType.MESH
F32 = jnp.float32
BF16 = jnp.bfloat16
SMEM = pltpu.SMEM
VMEM = pltpu.VMEM


def params(**kw):
    return pltpu.CompilerParams(vmem_limit_bytes=56 * 1024 * 1024, **kw)


def whole_block(shape):
    return pl.BlockSpec(shape, lambda *_: (0,) * len(shape))


def row_mask(count, slots):
    rows = lax.broadcasted_iota(jnp.int32, (slots, 1), 0)
    return jnp.where(rows < count, 1.0, 0.0).astype(F32)


def spread_body(step_cells, neigh, up, adj, local, remote, table):
    step = pl.program_id(0)
    blocks, slots = adj.shape[1], adj.shape[2]

    @pl.when(step == 0)
    def _():
        table[...] = jnp.zeros_like(table)

    for j in range(step_cells):
        cell = step * step_cells + j
        wide = jnp.concatenate([adj[j, k] for k in range(blocks)], axis=1)
        terms = lax.dot_general(wide, up[j], (((0,), (0,)), ((), ())), preferred_element_type=F32)
        for k in range(blocks):
            slot = neigh[cell, k]
            table[slot] = table[slot] + terms[k * slots : (k + 1) * slots]

    @pl.when(step == pl.num_programs(0) - 1)
    def _():
        cells = local.shape[0]
        local[...] = table[pl.ds(0, cells)]
        remote[...] = table[pl.ds(cells, remote.shape[0])].astype(BF16)


def spread(neigh, up, adjacency, received):
    cells, blocks, slots, _ = adjacency.shape
    part = up.shape[2]
    n = 4
    return pl.pallas_call(
        functools.partial(spread_body, n),
        grid=(cells // n,),
        in_specs=[
            pl.BlockSpec(memory_space=SMEM),
            pl.BlockSpec((n, slots, part), lambda i: (i, 0, 0)),
            pl.BlockSpec((n, blocks, slots, slots), lambda i: (i, 0, 0, 0)),
        ],
        out_specs=[whole_block((cells, slots, part)), whole_block((received, slots, part))],
        out_shape=[
            jax.ShapeDtypeStruct((cells, slots, part), F32),
            jax.ShapeDtypeStruct((received, slots, part), BF16),
        ],
        scratch_shapes=[VMEM((cells + received, slots, part), F32)],
        compiler_params=params(),
        cost_estimate=pl.CostEstimate(
            flops=2 * adjacency.size * part,
            bytes_accessed=30_000_000,
            transcendentals=0,
        ),
        name="spread",
    )(neigh, up, adjacency)


def greet(axes):
    barrier = pltpu.get_barrier_semaphore()
    expected = 0
    for axis in axes:
        size = lax.axis_size(axis)
        me = lax.axis_index(axis)
        for d in range(1, size):
            pl.semaphore_signal(
                barrier, inc=1, device_id={axis: lax.rem(me + d, size)}, device_id_type=MESH
            )
        expected += size - 1
    pl.semaphore_wait(barrier, expected)


def exchange_copies(axis, src, dst, sends, recvs):
    size = lax.axis_size(axis)
    me = lax.axis_index(axis)
    copies = []
    for d in range(1, size):
        peer = lax.rem(me + d, size)
        copies.append(
            pltpu.make_async_remote_copy(
                src_ref=src.at[peer],
                dst_ref=dst.at[me],
                send_sem=sends.at[d],
                recv_sem=recvs.at[d],
                device_id={axis: peer},
                device_id_type=MESH,
            )
        )
    copies.append(pltpu.make_async_copy(src.at[me], dst.at[me], recvs.at[0]))
    return copies


def start_all(copies):
    for copy in copies:
        copy.start()
    return copies


def wait_all(copies):
    for copy in copies:
        copy.wait()


def dma(*shape):
    return pltpu.SemaphoreType.DMA(shape)


def prepare_body(
    step_cells, occ, send, feat, adj, cot, scale_out, scaled_out, incoming, cot_in, outgoing, *sems
):
    step = pl.program_id(0)
    slots = adj.shape[2]
    sending = outgoing.shape[1]

    @pl.when(step == 0)
    def _():
        greet(("rep", "rows"))
        start_all(exchange_copies("rep", cot, cot_in, sems[0], sems[1]))

    for j in range(step_cells):
        cell = step * step_cells + j
        total = jnp.zeros((slots, slots), F32)
        for k in range(adj.shape[1]):
            a = adj[j, k].astype(F32)
            total += a * a
        scale = lax.rsqrt(jnp.sqrt(jnp.sum(total, axis=1, keepdims=True) + 1e-6))
        scale_out[j] = jnp.broadcast_to(scale, scale_out.shape[1:])
        keep = scale * row_mask(occ[cell], slots)
        scaled_out[cell] = (feat[j].astype(F32) * keep).astype(BF16)

    @pl.when(step == pl.num_programs(0) - 1)
    def _():
        def put(t, carry):
            peer, place = t // sending, t % sending
            outgoing[peer, place] = scaled_out[send[0, peer, place]]
            return carry

        lax.fori_loop(0, outgoing.shape[0] * sending, put, 0)
        copies = start_all(exchange_copies("rows", outgoing, incoming, sems[2], sems[3]))
        wait_all(copies)
        wait_all(exchange_copies("rep", cot, cot_in, sems[0], sems[1]))


def prepare(features, adjacency, occupancy, send, cot, collective_id):
    cells, blocks, slots, _ = adjacency.shape
    part = features.shape[2]
    n = 4
    _, peers, sending = send.shape
    table = (peers, sending, slots, part)
    reps = cot.shape[0]
    return pl.pallas_call(
        functools.partial(prepare_body, n),
        grid=(cells // n,),
        in_specs=[
            pl.BlockSpec(memory_space=SMEM),
            pl.BlockSpec(memory_space=SMEM),
            pl.BlockSpec((n, slots, part), lambda i: (i, 0, 0)),
            pl.BlockSpec((n, blocks, slots, slots), lambda i: (i, 0, 0, 0)),
            pl.BlockSpec(memory_space=pl.ANY),
        ],
        out_specs=[
            pl.BlockSpec((n, slots, part), lambda i: (i, 0, 0)),
            whole_block((cells, slots, part)),
            pl.BlockSpec(memory_space=pl.ANY),
            pl.BlockSpec(memory_space=pl.ANY),
        ],
        out_shape=[
            jax.ShapeDtypeStruct((cells, slots, part), F32),
            jax.ShapeDtypeStruct((cells, slots, part), BF16),
            jax.ShapeDtypeStruct(table, BF16),
            jax.ShapeDtypeStruct(cot.shape, BF16),
        ],
        scratch_shapes=[VMEM(table, BF16), dma(reps), dma(reps), dma(peers), dma(peers)],
        compiler_params=params(collective_id=collective_id, has_side_effects=True),
        name="prepare",
    )(occupancy, send, features, adjacency, cot)


def core_body(groups, neigh, occ, scaled_h, incoming_h, scale_h, adj_h, cot_h, weight_h, *refs):
    reps, rows, part = cot_h.shape
    up, outs, wgrads = refs[0], refs[1 : 1 + reps], refs[1 + reps : 1 + 2 * reps]
    table, scale, adj, cot, weight, agg, agg_in, slope_all, back_all, out_all, wgrad = refs[
        1 + 2 * reps : 12 + 2 * reps
    ]
    loads, adj_loads, send1, recv1, send2, recv2, stores = refs[12 + 2 * reps :]
    me = lax.axis_index("rep")
    cells, blocks, slots, _ = adj.shape
    per_rep = cells // reps
    per_group = per_rep // groups
    size = per_group * slots
    order = list(range(1, reps)) + [0]

    early = [
        pltpu.make_async_copy(scaled_h, table.at[pl.ds(0, cells)], loads.at[0]),
        pltpu.make_async_copy(
            incoming_h, table.at[pl.ds(cells, incoming_h.shape[0])], loads.at[1]
        ),
        pltpu.make_async_copy(scale_h, scale, loads.at[2]),
    ]
    start_all(early)
    adj_copies = {}
    for g in range(groups):
        for d in order:
            cell = lax.rem(me + d, reps) * per_rep + g * per_group
            span = pl.ds(cell, per_group)
            copy = pltpu.make_async_copy(adj_h.at[span], adj.at[span], adj_loads.at[g, d])
            copy.start()
            adj_copies[g, d] = copy
    late = start_all(
        [
            pltpu.make_async_copy(cot_h, cot, loads.at[3]),
            pltpu.make_async_copy(weight_h, weight, loads.at[4]),
        ]
    )
    greet(("rep",))
    wait_all(early)

    def copies_of(g, src, dst, sends, recvs):
        span = pl.ds(g * size, size)
        found = []
        for d in order:
            peer = lax.rem(me + d, reps)
            if d == 0:
                found.append(
                    pltpu.make_async_copy(src.at[me, span], dst.at[me, span], recvs.at[g, 0])
                )
                continue
            found.append(
                pltpu.make_async_remote_copy(
                    src_ref=src.at[peer, span],
                    dst_ref=dst.at[me, span],
                    send_sem=sends.at[g, d],
                    recv_sem=recvs.at[g, d],
                    device_id={"rep": peer},
                    device_id_type=MESH,
                )
            )
        return found

    forward = []
    for g in range(groups):
        copies = copies_of(g, agg, agg_in, send1, recv1)
        for i, d in enumerate(order):
            peer = lax.rem(me + d, reps)
            adj_copies[g, d].wait()
            for j in range(per_group):
                cell = peer * per_rep + g * per_group + j
                near = jnp.concatenate([table[neigh[cell, k]] for k in range(blocks)], axis=0)
                wide = jnp.concatenate([adj[cell, k] for k in range(blocks)], axis=1)
                total = jnp.dot(wide, near, preferred_element_type=F32)
                agg[peer, pl.ds(g * size + j * slots, slots)] = (total * scale[cell]).astype(BF16)
            copies[i].start()
        forward.append(copies)
    wait_all(late)
    backward = []
    for g in range(groups):
        wait_all(forward[g])
        span = pl.ds(g * size, size)
        base = me * per_rep + g * per_group
        a = jnp.concatenate([agg_in[q, span] for q in range(reps)], axis=1)
        pre = jnp.dot(a, weight[...], preferred_element_type=F32)
        mask = jnp.concatenate([row_mask(occ[base + j], slots) for j in range(per_group)], axis=0)
        sig = 0.5 * jnp.tanh(0.5 * pre) + 0.5
        o = (mask * (pre * sig)).astype(BF16)
        c = jnp.concatenate([cot[q, span] for q in range(reps)], axis=1).astype(F32)
        slope = (c * mask * sig * (1.0 + pre * (1.0 - sig))).astype(BF16)
        slope_all[span] = slope
        back = lax.dot_general(
            slope, weight[...], (((1,), (1,)), ((), ())), preferred_element_type=F32
        )
        s = scale[pl.ds(base, per_group)].reshape(size, part)
        for q in range(reps):
            cols = slice(q * part, (q + 1) * part)
            out_all[q, span] = o[:, cols]
            back_all[q, span] = (back[:, cols] * s).astype(BF16)
        backward += start_all(copies_of(g, back_all, up, send2, recv2))
    ends = []
    for d in range(reps):
        peer = lax.rem(me + d, reps)
        ends.append(pltpu.make_async_copy(out_all.at[peer], outs[d], stores.at[0, d]))
    start_all(ends)
    for q in range(reps):
        term = lax.dot_general(
            agg_in[q], slope_all[...], (((0,), (0,)), ((), ())), preferred_element_type=F32
        )
        wgrad[q] = term.astype(BF16)
    for d in range(reps):
        peer = lax.rem(me + d, reps)
        copy = pltpu.make_async_copy(wgrad.at[peer], wgrads[d], stores.at[1, d])
        copy.start()
        ends.append(copy)
    wait_all(ends)
    wait_all(backward)


def core(neigh, occupancy, scaled, incoming, scale, adjacency, cot, weight, collective_id):
    cells, _, slots, _ = adjacency.shape
    reps, rows, part = cot.shape
    groups = 4
    width = weight.shape[1]
    any_spec = pl.BlockSpec(memory_space=pl.ANY)
    results = pl.pallas_call(
        functools.partial(core_body, groups),
        in_specs=[pl.BlockSpec(memory_space=SMEM)] * 2 + [any_spec] * 6,
        out_specs=[any_spec] * (1 + 2 * reps),
        out_shape=[jax.ShapeDtypeStruct(cot.shape, BF16)]
        + [jax.ShapeDtypeStruct((rows, part), BF16)] * reps
        + [jax.ShapeDtypeStruct((part, width), BF16)] * reps,
        scratch_shapes=[
            VMEM((cells + incoming.shape[0], slots, part), BF16),
            VMEM(scale.shape, F32),
            VMEM(adjacency.shape, BF16),
            VMEM(cot.shape, BF16),
            VMEM(weight.shape, BF16),
            VMEM(cot.shape, BF16),
            VMEM(cot.shape, BF16),
            VMEM((rows, width), BF16),
            VMEM(cot.shape, BF16),
            VMEM(cot.shape, BF16),
            VMEM((reps, part, width), BF16),
            dma(5),
            dma(groups, reps),
            dma(groups, reps),
            dma(groups, reps),
            dma(groups, reps),
            dma(groups, reps),
            dma(2, reps),
        ],
        compiler_params=params(collective_id=collective_id, has_side_effects=True),
        name="core",
    )(neigh, occupancy, scaled, incoming, scale, adjacency, cot, weight)
    return results[0], results[1 : 1 + reps], results[1 + reps :]


def last_body(factor, cut, reps, terms, *refs):
    wgrads, returned, grad = refs[:reps], refs[reps], refs[reps + 1]
    rest = refs[reps + 2 :]
    greet(("rows",))
    peers = lax.axis_size("rows")
    me = lax.axis_index("rows")
    total = wgrads[0][...].astype(F32)
    for q in range(1, reps):
        total += wgrads[q][...].astype(F32)
    if not cut:
        grad[...] = total
        wait_all(start_all(exchange_copies("rows", terms, returned, rest[0], rest[1])))
        return
    held, parts = rest[2], rest[3]
    held[...] = total.astype(BF16).reshape(held.shape)
    sums = start_all(exchange_copies("rows", held, parts, rest[4], rest[5]))
    others = start_all(exchange_copies("rows", terms, returned, rest[0], rest[1]))
    wait_all(sums)
    total = parts[0].astype(F32)
    for p in range(1, peers):
        total += parts[p].astype(F32)
    grad[me] = total * factor
    copies = []
    for d in range(1, peers):
        copies.append(
            pltpu.make_async_remote_copy(
                src_ref=grad.at[me],
                dst_ref=grad.at[me],
                send_sem=rest[6].at[d],
                recv_sem=rest[7].at[d],
                device_id={"rows": lax.rem(me + d, peers)},
                device_id_type=MESH,
            )
        )
    wait_all(start_all(copies))
    wait_all(others)


def last_exchange(terms, wgrads, factor, collective_id):
    peers, reps = lax.axis_size("rows"), len(wgrads)
    part, width = wgrads[0].shape
    cut = part % (16 * peers) == 0
    scratch = [dma(peers), dma(peers)]
    grad_shape = (part, width)
    if cut:
        grad_shape = (peers, part // peers, width)
        scratch += [VMEM(grad_shape, BF16)] * 2 + [dma(peers)] * 4
    returned, grad = pl.pallas_call(
        functools.partial(last_body, factor, cut, reps),
        in_specs=[pl.BlockSpec(memory_space=pl.ANY)] + [pl.BlockSpec(memory_space=VMEM)] * reps,
        out_specs=[pl.BlockSpec(memory_space=pl.ANY), pl.BlockSpec(memory_space=VMEM)],
        out_shape=[
            jax.ShapeDtypeStruct(terms.shape, BF16),
            jax.ShapeDtypeStruct(grad_shape, F32),
        ],
        scratch_shapes=scratch,
        compiler_params=params(collective_id=collective_id, has_side_effects=True),
        name="last_exchange",
    )(terms, *wgrads)
    if not cut:
        grad = lax.psum(grad, "rows") * factor
    return returned, grad.reshape(part, width)


def combine_body(reps, send, occ, local, returned, scale, *refs):
    parts, out, output, total, sems = refs[:reps], *refs[reps:]
    me = lax.axis_index("rep")
    slots = local.shape[1]
    sending = returned.shape[1]
    moves = []
    for d in range(reps):
        place = lax.rem(me + (reps - d), reps)
        moves.append(pltpu.make_async_copy(parts[d], output.at[place], sems.at[d]))
    start_all(moves)
    total[...] = local[...]

    def add(t, carry):
        peer, place = t // sending, t % sending
        cell = send[0, peer, place]
        total[cell] = total[cell] + returned[peer, place].astype(F32)
        return carry

    lax.fori_loop(0, returned.shape[0] * sending, add, 0)

    def finish(i, carry):
        out[i] = (total[i] * (scale[i] * row_mask(occ[i], slots))).astype(BF16)
        return carry

    lax.fori_loop(0, local.shape[0], finish, 0)
    wait_all(moves)


def combine(send, occupancy, local, returned, scale, parts):
    reps = len(parts)
    vmem, hbm = pl.BlockSpec(memory_space=VMEM), pl.BlockSpec(memory_space=pl.ANY)
    return pl.pallas_call(
        functools.partial(combine_body, reps),
        in_specs=[pl.BlockSpec(memory_space=SMEM)] * 2 + [vmem] * 3 + [hbm] * reps,
        out_specs=[vmem, hbm],
        out_shape=[
            jax.ShapeDtypeStruct(local.shape, BF16),
            jax.ShapeDtypeStruct((reps,) + parts[0].shape, BF16),
        ],
        scratch_shapes=[VMEM(local.shape, F32), dma(reps)],
        compiler_params=params(),
        name="combine",
    )(send, occupancy, local, returned, scale, *parts)


def shifted(blocks):
    reps = len(blocks)
    moved = [blocks[0]]
    for d in range(1, reps):
        moved.append(lax.ppermute(blocks[d], "rep", [(i, (i + d) % reps) for i in range(reps)]))
    return moved


def on_device(features, adjacency, neighbours, occupancy, send_cells, weight, cotangent):
    cells, _, slots, _ = adjacency.shape
    part = features.shape[1]
    peers, reps = lax.axis_size("rows"), lax.axis_size("rep")
    sending = send_cells.shape[2]
    rows = cells * slots
    cell_shape = (cells, slots, part)
    cot = cotangent.reshape(reps, rows // reps, part)

    scale, scaled, incoming, cot_rows = prepare(
        features.reshape(cell_shape), adjacency, occupancy, send_cells, cot, 1
    )
    up, outs, wgrads = core(
        neighbours,
        occupancy,
        scaled,
        incoming.reshape(-1, slots, part),
        scale,
        adjacency,
        cot_rows,
        weight,
        2,
    )
    wgrads = shifted(wgrads)
    outs = shifted(outs)
    local, remote = spread(neighbours, up.reshape(cell_shape), adjacency, peers * sending)
    returned, weight_grad = last_exchange(
        remote.reshape(peers, sending, slots, part), wgrads, float(rows * peers) ** (-0.5), 3
    )
    feature_grad, output = combine(send_cells, occupancy, local, returned, scale, outs)
    return output.reshape(rows, part), weight_grad, feature_grad.reshape(rows, part)


def solution(mesh):
    placed = (
        P("rows", "rep"),
        P("rows", None, None, None),
        P("rows", None),
        P("rows"),
        P("rows", None, None),
        P(),
        P("rows", "rep"),
    )
    return jax.shard_map(
        on_device,
        mesh=mesh,
        in_specs=placed,
        out_specs=(P("rows", "rep"), P("rep", None), P("rows", "rep")),
        check_vma=False,
    )
```

time: 336 us -> 142 us (0.42)
  waiting for transfers between devices: 190 us -> 5.19 us
  Pallas kernels: 0 us -> 126 us
  other arithmetic: 56.1 us -> 0 us
  matrix products: 28.9 us -> 0 us
  local copies, waits for them, and re-layouts: 32.4 us -> 4.96 us
  between operations: 13.9 us -> 0.73 us
  starting transfers between devices: 13.1 us -> 4.06 us
    pallas_call x0 -> x5, Pallas kernels: none -> 126 us  [the longest x1 36.3 us: combine(): pl.pallas_call(functools.partial(combine_body, reps), in_specs=[pl.BlockS...]
    reduce_scatter x1 -> x0, waiting for transfers between devices: 70.7 us -> none  [on_device(): lax.psum_scatter(partial_terms, 'rep', scatter_dimension=1, tiled=True)]
    psum x1 -> x0, waiting for transfers between devices: 70.6 us -> none  [on_device(): weight_grad = lax.psum(grad_rows, 'rows') * float(total_rows) ** (-0.5)]
    scatter-add x2 -> x0, other arithmetic: 42.2 us -> none  [the longest x1 39.6 us: on_device(): jax.ops.segment_sum(contrib.reshape(cells * blocks, slots_cell, part), ne...]
    all_gather x1 -> x0, waiting for transfers between devices: 35 us -> none  [on_device(): piece = lax.all_gather(slope, 'rep', axis=1, tiled=True)]
    dot_general x5 -> x0, matrix products: 28.9 us -> none  [the longest x1 9.69 us: on_device(): jnp.einsum('ikrc,irf->ikcf', adjacency, upstream, preferred_element_type=...]
    reshape x2 -> x0, local copies, waits for them, and re-layouts: 15.5 us -> none  [the longest x1 12.6 us: on_device(): contrib.reshape(cells * blocks, slots_cell, part)]
    all_to_all x2 -> x0, waiting for transfers between devices: 14.2 us -> none  [the longest x1 14.2 us: on_device(): lax.all_to_all(outgoing, 'rows', split_axis=0, concat_axis=0, tiled=True)]
  transfers between devices with their start and end apart: 5 -> 6, of which waited for: 4 -> 2; matrix products, arithmetic and copies ran while one was open for 2% -> 0% of each run, Pallas kernels for 0% -> 27%
where the time goes in v2:
time: 142 us; the launch traced here: 141 us
  Pallas kernels  126 us (89%)
  waiting for transfers between devices  5.19 us (4%)
  local copies, waits for them, and re-layouts  4.96 us (3%)
  starting transfers between devices  4.06 us (3%)
    pallas_call x1, Pallas kernels, combine(): pl.pallas_call(functools.partial(combine_body, reps), in_specs=[pl.BlockS...  36.3 us
    pallas_call x1, Pallas kernels, core(): pl.pallas_call(functools.partial(core_body, groups), in_specs=[pl.BlockSp...  28.8 us
    pallas_call x1, Pallas kernels, last_exchange(): pl.pallas_call(functools.partial(last_body, factor, cut, reps), in_specs=...  28.2 us
    pallas_call x1, Pallas kernels, prepare(): pl.pallas_call(functools.partial(prepare_body, n), grid=(cells // n,), in...  23.8 us
    pallas_call x1, Pallas kernels, spread(): pl.pallas_call(functools.partial(spread_body, n), grid=(cells // n,), in_...  9.22 us
    ppermute x6, waiting for transfers between devices, shifted(): lax.ppermute(blocks[d], 'rep', [(i, (i + d) % reps) for i in range(reps)])  5.19 us
    unnamed x17, local copies, waits for them, and re-layouts  4.96 us
    ppermute x6, starting transfers between devices, shifted(): lax.ppermute(blocks[d], 'rep', [(i, (i + d) % reps) for i in range(reps)])  4.06 us
  transfers between devices with their start and end apart: 6, of which 2 were waited for; matrix products, arithmetic and copies ran while one was open for 0% of the time, Pallas kernels for 27%

profile of v2, /device:TPU:0, one launch (start us, length us, event | category | flops | bytes accessed | tf_op | source)
XLA Modules:
  0.0 141.3 jit_solution(1728395238338176085)
XLA Ops:
  0.6 1.3 copy.13.send
  2.0 1.4 copy.12.neigh
  3.3 23.8 %prepare.1 = (f32[32,128,128]{2,1,0:T(8,128)}, bf16[32,128,128]{2,1,0:T(8,128)(2,1)}, bf16[8,2,128,128]{3,2,1,0:T(8,128)(2,1)}, bf16[4,1024,128]{2,1,0:T(8,128)(2,1)}) custom-call(s32[32]{0:T(128)} %occ.5, s32[1,8,2]{2,1,0:T(8,128)} %copy.13.send, bf16[32,128,128]{2,1,0:T(8,128)(2,1)} %bitcast.9, bf16[32,6,128,128]{3,2,1,0:T(8,128)(2,1)} %adj.3, ...), custom_call_target="tpu_custom_call" | custom-call | tf_op jit(solution)/shard_map/prepare/pallas_call | solution.py:173
  27.1 28.8 %core.1 = (bf16[4,1024,128]{2,1,0:T(8,128)(2,1)}, bf16[1024,128]{1,0:T(8,128)(2,1)}, bf16[1024,128]{1,0:T(8,128)(2,1)}, bf16[1024,128]{1,0:T(8,128)(2,1)}, bf16[...) custom-call(s32[32,6]{1,0:T(8,128)} %copy.12.neigh, ...), custom_call_target="tpu_custom_call" | custom-call | tf_op jit(solution)/shard_map/core/pallas_call | solution.py:324
  55.9 0.6 collective-permute-start
  56.5 0.1 collective-permute-start.3
  56.5 1.6 %collective-permute-start.4 = (bf16[1024,128]{1,0:T(8,128)(2,1)}, bf16[1024,128]{1,0:T(8,128)(2,1)S(1)}, u32[]{:S(2)}, u32[]{:S(2)}) collective-permute-start(bf16[1024,128]{1,0:T(8,128)(2,1)} %get-tuple-element.36), channel_id=1, source_target_pairs={{0,2},{1,3},{2,0},{3,1},{4,6},{5,7},{6,4},{7,5},{8,10},{9,11},{10,... | collective-permute-start | bytes 786440 | tf_op jit(solution)/shard_map/ppermute | solution.py:470
  58.1 0.2 collective-permute-start.5
  58.3 1.7 %collective-permute-start.1 = (bf16[128,512]{1,0:T(8,128)(2,1)}, bf16[128,512]{1,0:T(8,128)(2,1)S(1)}, u32[]{:S(2)}, u32[]{:S(2)}) collective-permute-start(bf16[128,512]{1,0:T(8,128)(2,1)} %get-tuple-element.31), channel_id=1, source_target_pairs={{0,2},{1,3},{2,0},{3,1},{4,6},{5,7},{6,4},{7,5},{8,10},{9,11},{10,... | collective-permute-start | bytes 393224 | tf_op jit(solution)/shard_map/ppermute | solution.py:470
  60.0 0.8 collective-permute-done.refs_1_
  60.8 0.0 copy-start.4
  60.8 0.0 collective-permute-start.2
  60.8 9.2 %spread.1 = (f32[32,128,128]{2,1,0:T(8,128)}, bf16[16,128,128]{2,1,0:T(8,128)(2,1)}) custom-call(s32[32,6]{1,0:T(8,128)} %copy.12.neigh, bf16[32,128,128]{2,1,0:T(8,128)(2,1)} %bitcast.8, bf16[32,6,128,128]{3,2,1,0:T(8,128)(2,1)} %adj.3), custom_call_target="tpu_custom_call" | custom-call | flops 805306368 | bytes 30000000 | tf_op jit(solution)/shard_map/spread/pallas_call | solution.py:57
  70.0 0.0 copy-done.4
  70.0 4.4 %collective-permute-done.1.refs_2_ = bf16[128,512]{1,0:T(8,128)(2,1)S(1)} collective-permute-done((bf16[128,512]{1,0:T(8,128)(2,1)}, bf16[128,512]{1,0:T(8,128)(2,1)S(1)}, u32[]{:S(2)}, u32[]{:S(2)}) %collective-permute-start.1) | collective-permute-done | bytes 131104 | tf_op jit(solution)/shard_map/ppermute | solution.py:470
  74.4 0.0 copy-start.5
  74.4 0.0 collective-permute-done.2.refs_3_
  74.4 0.0 copy-start.6
  74.4 0.6 copy-done.5
  75.0 0.0 copy-done.6
  75.1 28.2 %last_exchange.1 = (bf16[8,2,128,128]{3,2,1,0:T(8,128)(2,1)}, f32[8,16,512]{2,1,0:T(8,128)}) custom-call(bf16[8,2,128,128]{3,2,1,0:T(8,128)(2,1)} %bitcast.12, bf16[128,512]{1,0:T(8,128)(2,1)} %get-tuple-element.29.refs_0_, bf16[128,512]{1,0:T(8,128)(2,1)} %copy-done.4, bf16[128,512]{1,0:T(8,128)(2,1)} %copy-done.5, bf16[128,512]{1,0:T(8,128)(2,1)} %copy-done.6), custom_call_target="tpu_custom_call" | custom-call | tf_op jit(solution)/shard_map/last_exchange/pallas_call | solution.py:404
  103.3 0.0 collective-permute-done.3.refs_1_
  103.3 0.0 copy-start.1
  103.3 0.0 collective-permute-done.4.refs_2_
  103.3 0.0 copy-start.2
  103.4 0.0 collective-permute-done.5.refs_3_
  103.4 0.0 copy-start.3
  103.4 0.7 copy-done.1
  104.0 0.1 copy-done.2
  104.1 0.1 copy-done.3
  104.2 0.0 copy-start
  104.2 36.3 %combine.1 = (bf16[32,128,128]{2,1,0:T(8,128)(2,1)}, bf16[4,1024,128]{2,1,0:T(8,128)(2,1)}) custom-call(s32[1,8,2]{2,1,0:T(8,128)} %copy.13.send, s32[32]{0:T(128)} %occ.5, f32[32,128,128]{2,1,0:T(8,128)} %get-tuple-element.27.local, bf16[8,2,128,128]{3,2,1,0:T(8,128)(2,1)} %get-tuple-element.33.returned, f32[32,128,128]{2,1,0:T(8,128)} %get-tuple-element.24.scale_h.scale, ...), custom_call_target="tpu_custom_call" | custom-call | tf_op jit(solution)/shard_map/combine/pallas_call | solution.py:452
  140.6 0.0 copy-done
  140.6 0.7 copy.15
Async XLA Ops:
  55.9 4.9 %collective-permute-start = (bf16[128,512]{1,0:T(8,128)(2,1)}, bf16[128,512]{1,0:T(8,128)(2,1)S(1)}, u32[]{:S(2)}, u32[]{:S(2)}) collective-permute-start(bf16[128,512]{1,0:T(8,128)(2,1)} %get-tuple-element.30), channel_id=1, source_target_pairs={{0,1},{1,2},{2,3},{3,0},{4,5},{5,6},{6,7},{7,4},{8,9},{9,10},{10,1... | collective-permute-start | bytes 393224 | tf_op jit(solution)/shard_map/ppermute | solution.py:470
  56.5 46.8 %collective-permute-start.3 = (bf16[1024,128]{1,0:T(8,128)(2,1)}, bf16[1024,128]{1,0:T(8,128)(2,1)S(1)}, u32[]{:S(2)}, u32[]{:S(2)}) collective-permute-start(bf16[1024,128]{1,0:T(8,128)(2,1)} %get-tuple-element.35), channel_id=1, source_target_pairs={{0,1},{1,2},{2,3},{3,0},{4,5},{5,6},{6,7},{7,4},{8,9},{9,10},{10,1... | collective-permute-start | bytes 786440 | tf_op jit(solution)/shard_map/ppermute | solution.py:470
  56.5 46.8 %collective-permute-start.4 = (bf16[1024,128]{1,0:T(8,128)(2,1)}, bf16[1024,128]{1,0:T(8,128)(2,1)S(1)}, u32[]{:S(2)}, u32[]{:S(2)}) collective-permute-start(bf16[1024,128]{1,0:T(8,128)(2,1)} %get-tuple-element.36), channel_id=1, source_target_pairs={{0,2},{1,3},{2,0},{3,1},{4,6},{5,7},{6,4},{7,5},{8,10},{9,11},{10,... | collective-permute-start | bytes 786440 | tf_op jit(solution)/shard_map/ppermute | solution.py:470
  58.1 45.3 %collective-permute-start.5 = (bf16[1024,128]{1,0:T(8,128)(2,1)}, bf16[1024,128]{1,0:T(8,128)(2,1)S(1)}, u32[]{:S(2)}, u32[]{:S(2)}) collective-permute-start(bf16[1024,128]{1,0:T(8,128)(2,1)} %get-tuple-element.37), channel_id=1, source_target_pairs={{0,3},{1,0},{2,1},{3,2},{4,7},{5,4},{6,5},{7,6},{8,11},{9,8},{10,9... | collective-permute-start | bytes 786440 | tf_op jit(solution)/shard_map/ppermute | solution.py:470
  58.3 16.1 %collective-permute-start.1 = (bf16[128,512]{1,0:T(8,128)(2,1)}, bf16[128,512]{1,0:T(8,128)(2,1)S(1)}, u32[]{:S(2)}, u32[]{:S(2)}) collective-permute-start(bf16[128,512]{1,0:T(8,128)(2,1)} %get-tuple-element.31), channel_id=1, source_target_pairs={{0,2},{1,3},{2,0},{3,1},{4,6},{5,7},{6,4},{7,5},{8,10},{9,11},{10,... | collective-permute-start | bytes 393224 | tf_op jit(solution)/shard_map/ppermute | solution.py:470
  60.8 9.2 %copy-start.4 = (bf16[128,512]{1,0:T(8,128)(2,1)}, bf16[128,512]{1,0:T(8,128)(2,1)S(1)}, u32[]{:S(2)}) copy-start(bf16[128,512]{1,0:T(8,128)(2,1)S(1)} %collective-permute-done.refs_1_) | copy-start | bytes 393220
  60.8 13.6 %collective-permute-start.2 = (bf16[128,512]{1,0:T(8,128)(2,1)}, bf16[128,512]{1,0:T(8,128)(2,1)S(1)}, u32[]{:S(2)}, u32[]{:S(2)}) collective-permute-start(bf16[128,512]{1,0:T(8,128)(2,1)} %get-tuple-element.32), channel_id=1, source_target_pairs={{0,3},{1,0},{2,1},{3,2},{4,7},{5,4},{6,5},{7,6},{8,11},{9,8},{10,9... | collective-permute-start | bytes 393224 | tf_op jit(solution)/shard_map/ppermute | solution.py:470
  74.4 0.7 copy-start.5
  74.4 0.7 copy-start.6
  103.3 0.7 copy-start.1
  103.3 0.8 copy-start.2
  103.4 0.9 copy-start.3
  104.2 36.3 %copy-start = (f32[8,16,512]{2,1,0:T(8,128)S(1)}, f32[8,16,512]{2,1,0:T(8,128)}, u32[]{:S(2)}) copy-start(f32[8,16,512]{2,1,0:T(8,128)} %get-tuple-element.39) | copy-start | bytes 786436

commit v3 on v2

--- a/solution.py
+++ b/solution.py
@@ -178,7 +178,7 @@
             pl.BlockSpec(memory_space=SMEM),
             pl.BlockSpec((n, slots, part), lambda i: (i, 0, 0)),
             pl.BlockSpec((n, blocks, slots, slots), lambda i: (i, 0, 0, 0)),
-            pl.BlockSpec(memory_space=pl.ANY),
+            pl.BlockSpec(memory_space=VMEM),
         ],
         out_specs=[
             pl.BlockSpec((n, slots, part), lambda i: (i, 0, 0)),
@@ -200,11 +200,9 @@
 
 def core_body(groups, neigh, occ, scaled_h, incoming_h, scale_h, adj_h, cot_h, weight_h, *refs):
     reps, rows, part = cot_h.shape
-    up, outs, wgrads = refs[0], refs[1 : 1 + reps], refs[1 + reps : 1 + 2 * reps]
-    table, scale, adj, cot, weight, agg, agg_in, slope_all, back_all, out_all, wgrad = refs[
-        1 + 2 * reps : 12 + 2 * reps
-    ]
-    loads, adj_loads, send1, recv1, send2, recv2, stores = refs[12 + 2 * reps :]
+    up, out_all, wgrad = refs[:3]
+    table, scale, adj, cot, weight, agg, agg_in, slope_all, back_all = refs[3:12]
+    loads, adj_loads, send1, recv1, send2, recv2 = refs[12:]
     me = lax.axis_index("rep")
     cells, blocks, slots, _ = adj.shape
     per_rep = cells // reps
@@ -296,22 +294,11 @@
             out_all[q, span] = o[:, cols]
             back_all[q, span] = (back[:, cols] * s).astype(BF16)
         backward += start_all(copies_of(g, back_all, up, send2, recv2))
-    ends = []
-    for d in range(reps):
-        peer = lax.rem(me + d, reps)
-        ends.append(pltpu.make_async_copy(out_all.at[peer], outs[d], stores.at[0, d]))
-    start_all(ends)
     for q in range(reps):
         term = lax.dot_general(
             agg_in[q], slope_all[...], (((0,), (0,)), ((), ())), preferred_element_type=F32
         )
         wgrad[q] = term.astype(BF16)
-    for d in range(reps):
-        peer = lax.rem(me + d, reps)
-        copy = pltpu.make_async_copy(wgrad.at[peer], wgrads[d], stores.at[1, d])
-        copy.start()
-        ends.append(copy)
-    wait_all(ends)
     wait_all(backward)
 
 
@@ -321,13 +308,15 @@
     groups = 4
     width = weight.shape[1]
     any_spec = pl.BlockSpec(memory_space=pl.ANY)
-    results = pl.pallas_call(
+    return pl.pallas_call(
         functools.partial(core_body, groups),
         in_specs=[pl.BlockSpec(memory_space=SMEM)] * 2 + [any_spec] * 6,
-        out_specs=[any_spec] * (1 + 2 * reps),
-        out_shape=[jax.ShapeDtypeStruct(cot.shape, BF16)]
-        + [jax.ShapeDtypeStruct((rows, part), BF16)] * reps
-        + [jax.ShapeDtypeStruct((part, width), BF16)] * reps,
+        out_specs=[any_spec] + [pl.BlockSpec(memory_space=VMEM)] * 2,
+        out_shape=[
+            jax.ShapeDtypeStruct(cot.shape, BF16),
+            jax.ShapeDtypeStruct(cot.shape, BF16),
+            jax.ShapeDtypeStruct((reps, part, width), BF16),
+        ],
         scratch_shapes=[
             VMEM((cells + incoming.shape[0], slots, part), BF16),
             VMEM(scale.shape, F32),
@@ -338,40 +327,36 @@
             VMEM(cot.shape, BF16),
             VMEM((rows, width), BF16),
             VMEM(cot.shape, BF16),
-            VMEM(cot.shape, BF16),
-            VMEM((reps, part, width), BF16),
             dma(5),
             dma(groups, reps),
             dma(groups, reps),
             dma(groups, reps),
             dma(groups, reps),
             dma(groups, reps),
-            dma(2, reps),
         ],
         compiler_params=params(collective_id=collective_id, has_side_effects=True),
         name="core",
     )(neigh, occupancy, scaled, incoming, scale, adjacency, cot, weight)
-    return results[0], results[1 : 1 + reps], results[1 + reps :]
-
-
-def last_body(factor, cut, reps, terms, *refs):
-    wgrads, returned, grad = refs[:reps], refs[reps], refs[reps + 1]
-    rest = refs[reps + 2 :]
-    greet(("rows",))
+
+
+def last_body(factor, cut, terms, out_rows, wgrad, returned, out, grad, ph1, *sems):
+    greet(("rep", "rows"))
     peers = lax.axis_size("rows")
     me = lax.axis_index("rows")
-    total = wgrads[0][...].astype(F32)
-    for q in range(1, reps):
-        total += wgrads[q][...].astype(F32)
+    first = start_all(exchange_copies("rep", wgrad, ph1, sems[0], sems[1]))
+    others = start_all(exchange_copies("rows", terms, returned, sems[2], sems[3]))
+    wait_all(first)
+    others += start_all(exchange_copies("rep", out_rows, out, sems[4], sems[5]))
+    total = ph1[0].astype(F32)
+    for q in range(1, ph1.shape[0]):
+        total += ph1[q].astype(F32)
     if not cut:
         grad[...] = total
-        wait_all(start_all(exchange_copies("rows", terms, returned, rest[0], rest[1])))
+        wait_all(others)
         return
-    held, parts = rest[2], rest[3]
+    held, parts = sems[6], sems[7]
     held[...] = total.astype(BF16).reshape(held.shape)
-    sums = start_all(exchange_copies("rows", held, parts, rest[4], rest[5]))
-    others = start_all(exchange_copies("rows", terms, returned, rest[0], rest[1]))
-    wait_all(sums)
+    wait_all(start_all(exchange_copies("rows", held, parts, sems[8], sems[9])))
     total = parts[0].astype(F32)
     for p in range(1, peers):
         total += parts[p].astype(F32)
@@ -382,8 +367,8 @@
             pltpu.make_async_remote_copy(
                 src_ref=grad.at[me],
                 dst_ref=grad.at[me],
-                send_sem=rest[6].at[d],
-                recv_sem=rest[7].at[d],
+                send_sem=sems[10].at[d],
+                recv_sem=sems[11].at[d],
                 device_id={"rows": lax.rem(me + d, peers)},
                 device_id_type=MESH,
             )
@@ -392,42 +377,37 @@
     wait_all(others)
 
 
-def last_exchange(terms, wgrads, factor, collective_id):
-    peers, reps = lax.axis_size("rows"), len(wgrads)
-    part, width = wgrads[0].shape
+def last_exchange(terms, out_rows, wgrad, factor, collective_id):
+    peers = lax.axis_size("rows")
+    reps, part, width = wgrad.shape
     cut = part % (16 * peers) == 0
-    scratch = [dma(peers), dma(peers)]
+    scratch = [VMEM(wgrad.shape, BF16)] + [dma(reps)] * 2 + [dma(peers)] * 2 + [dma(reps)] * 2
     grad_shape = (part, width)
     if cut:
         grad_shape = (peers, part // peers, width)
         scratch += [VMEM(grad_shape, BF16)] * 2 + [dma(peers)] * 4
-    returned, grad = pl.pallas_call(
-        functools.partial(last_body, factor, cut, reps),
-        in_specs=[pl.BlockSpec(memory_space=pl.ANY)] + [pl.BlockSpec(memory_space=VMEM)] * reps,
-        out_specs=[pl.BlockSpec(memory_space=pl.ANY), pl.BlockSpec(memory_space=VMEM)],
+    vmem = pl.BlockSpec(memory_space=VMEM)
+    returned, out, grad = pl.pallas_call(
+        functools.partial(last_body, factor, cut),
+        in_specs=[vmem] * 3,
+        out_specs=[vmem, pl.BlockSpec(memory_space=pl.ANY), vmem],
         out_shape=[
             jax.ShapeDtypeStruct(terms.shape, BF16),
+            jax.ShapeDtypeStruct(out_rows.shape, BF16),
             jax.ShapeDtypeStruct(grad_shape, F32),
         ],
         scratch_shapes=scratch,
         compiler_params=params(collective_id=collective_id, has_side_effects=True),
         name="last_exchange",
-    )(terms, *wgrads)
+    )(terms, out_rows, wgrad)
     if not cut:
         grad = lax.psum(grad, "rows") * factor
-    return returned, grad.reshape(part, width)
-
-
-def combine_body(reps, send, occ, local, returned, scale, *refs):
-    parts, out, output, total, sems = refs[:reps], *refs[reps:]
-    me = lax.axis_index("rep")
+    return returned, out, grad.reshape(part, width)
+
+
+def combine_body(send, occ, local, returned, scale, out, total):
     slots = local.shape[1]
     sending = returned.shape[1]
-    moves = []
-    for d in range(reps):
-        place = lax.rem(me + (reps - d), reps)
-        moves.append(pltpu.make_async_copy(parts[d], output.at[place], sems.at[d]))
-    start_all(moves)
     total[...] = local[...]
 
     def add(t, carry):
@@ -443,32 +423,19 @@
         return carry
 
     lax.fori_loop(0, local.shape[0], finish, 0)
-    wait_all(moves)
-
-
-def combine(send, occupancy, local, returned, scale, parts):
-    reps = len(parts)
-    vmem, hbm = pl.BlockSpec(memory_space=VMEM), pl.BlockSpec(memory_space=pl.ANY)
+
+
+def combine(send, occupancy, local, returned, scale):
+    vmem = pl.BlockSpec(memory_space=VMEM)
     return pl.pallas_call(
-        functools.partial(combine_body, reps),
-        in_specs=[pl.BlockSpec(memory_space=SMEM)] * 2 + [vmem] * 3 + [hbm] * reps,
-        out_specs=[vmem, hbm],
-        out_shape=[
-            jax.ShapeDtypeStruct(local.shape, BF16),
-            jax.ShapeDtypeStruct((reps,) + parts[0].shape, BF16),
-        ],
-        scratch_shapes=[VMEM(local.shape, F32), dma(reps)],
+        combine_body,
+        in_specs=[pl.BlockSpec(memory_space=SMEM)] * 2 + [vmem] * 3,
+        out_specs=vmem,
+        out_shape=jax.ShapeDtypeStruct(local.shape, BF16),
+        scratch_shapes=[VMEM(local.shape, F32)],
         compiler_params=params(),
         name="combine",
-    )(send, occupancy, local, returned, scale, *parts)
-
-
-def shifted(blocks):
-    reps = len(blocks)
-    moved = [blocks[0]]
-    for d in range(1, reps):
-        moved.append(lax.ppermute(blocks[d], "rep", [(i, (i + d) % reps) for i in range(reps)]))
-    return moved
+    )(send, occupancy, local, returned, scale)
 
 
 def on_device(features, adjacency, neighbours, occupancy, send_cells, weight, cotangent):
@@ -483,7 +450,7 @@
     scale, scaled, incoming, cot_rows = prepare(
         features.reshape(cell_shape), adjacency, occupancy, send_cells, cot, 1
     )
-    up, outs, wgrads = core(
+    up, out_rows, wgrad = core(
         neighbours,
         occupancy,
         scaled,
@@ -494,13 +461,15 @@
         weight,
         2,
     )
-    wgrads = shifted(wgrads)
-    outs = shifted(outs)
     local, remote = spread(neighbours, up.reshape(cell_shape), adjacency, peers * sending)
-    returned, weight_grad = last_exchange(
-        remote.reshape(peers, sending, slots, part), wgrads, float(rows * peers) ** (-0.5), 3
-    )
-    feature_grad, output = combine(send_cells, occupancy, local, returned, scale, outs)
+    returned, output, weight_grad = last_exchange(
+        remote.reshape(peers, sending, slots, part),
+        out_rows,
+        wgrad,
+        float(rows * peers) ** (-0.5),
+        3,
+    )
+    feature_grad = combine(send_cells, occupancy, local, returned, scale)
     return output.reshape(rows, part), weight_grad, feature_grad.reshape(rows, part)
 
 

time: 142 us -> 104 us (0.73)
  Pallas kernels: 126 us -> 98.3 us
  waiting for transfers between devices: 5.19 us -> 0 us
  starting transfers between devices: 4.06 us -> 0 us
    pallas_call x2, Pallas kernels: 64.6 us -> 35.2 us  [the longest x1 30.8 us: last_exchange(): pl.pallas_call(functools.partial(last_body, factor, cut), in_specs=[vmem]...]
    ppermute x6 -> x0, waiting for transfers between devices: 5.19 us -> none  [shifted(): lax.ppermute(blocks[d], 'rep', [(i, (i + d) % reps) for i in range(reps)])]
    ppermute x6 -> x0, starting transfers between devices: 4.06 us -> none  [shifted(): lax.ppermute(blocks[d], 'rep', [(i, (i + d) % reps) for i in range(reps)])]
    unnamed x17 -> x8, local copies, waits for them, and re-layouts: 4.96 us -> 4.51 us
  transfers between devices with their start and end apart: 6 -> 0, of which waited for: 2 -> 0; matrix products, arithmetic and copies ran while one was open for 0% -> 0% of each run, Pallas kernels for 27% -> 0%
where the time goes in v3:
time: 104 us; the launch traced here: 103 us
  Pallas kernels  98.3 us (95%)
  local copies, waits for them, and re-layouts  4.51 us (4%)
    pallas_call x1, Pallas kernels, last_exchange(): pl.pallas_call(functools.partial(last_body, factor, cut), in_specs=[vmem]...  30.8 us
    pallas_call x1, Pallas kernels, core(): pl.pallas_call(functools.partial(core_body, groups), in_specs=[pl.BlockSp...  29.8 us
    pallas_call x1, Pallas kernels, prepare(): pl.pallas_call(functools.partial(prepare_body, n), grid=(cells // n,), in...  24.1 us
    pallas_call x1, Pallas kernels, spread(): pl.pallas_call(functools.partial(spread_body, n), grid=(cells // n,), in_...  9.2 us
    unnamed x8, local copies, waits for them, and re-layouts  4.51 us
    pallas_call x1, Pallas kernels, combine(): pl.pallas_call(combine_body, in_specs=[pl.BlockSpec(memory_space=SMEM)] *...  4.43 us

profile of v3, /device:TPU:0, one launch (start us, length us, event | category | flops | bytes accessed | tf_op | source)
XLA Modules:
  0.0 103.5 jit_solution(2529678548797391745)
XLA Ops:
  0.6 1.3 %copy.10.send = s32[1,8,2]{2,1,0:T(8,128)} copy(s32[1,8,2]{1,2,0:T(2,128)} %param.11) | data formatting | bytes 128 | tf_op args[4]
  2.0 1.4 %copy.12.neigh = s32[32,6]{1,0:T(8,128)} copy(s32[32,6]{0,1:T(8,128)} %param.9) | data formatting | bytes 1536 | tf_op args[2]
  3.3 24.1 %prepare.1 = (f32[32,128,128]{2,1,0:T(8,128)}, bf16[32,128,128]{2,1,0:T(8,128)(2,1)}, bf16[8,2,128,128]{3,2,1,0:T(8,128)(2,1)}, bf16[4,1024,128]{2,1,0:T(8,128)(2,1)}) custom-call(s32[32]{0:T(128)} %occ.5, s32[1,8,2]{2,1,0:T(8,128)} %copy.10.send, bf16[32,128,128]{2,1,0:T(8,128)(2,1)} %bitcast.11, bf16[32,6,128,128]{3,2,1,0:T(8,128)(2,1)} %adj.3, ...), custom_call_target="tpu_custom_call" | custom-call | tf_op jit(solution)/shard_map/prepare/pallas_call | solution.py:173
  27.4 29.8 %core.1 = (bf16[4,1024,128]{2,1,0:T(8,128)(2,1)}, bf16[4,1024,128]{2,1,0:T(8,128)(2,1)}, bf16[4,128,512]{2,1,0:T(8,128)(2,1)}) custom-call(s32[32,6]{1,0:T(8,128)} %copy.12.neigh, s32[32]{0:T(128)} %occ.5, bf16[32,128,128]{2,1,0:T(8,128)(2,1)} %get-tuple-element.15.scaled_h, bf16[16,128,128]{2,1,0:T(8,128)(2,1)} %bitcast.13, ...), custom_call_target="tpu_custom_call" | custom-call | tf_op jit(solution)/shard_map/core/pallas_call | solution.py:311
  57.3 9.2 %spread.1 = (f32[32,128,128]{2,1,0:T(8,128)}, bf16[16,128,128]{2,1,0:T(8,128)(2,1)}) custom-call(s32[32,6]{1,0:T(8,128)} %copy.12.neigh, bf16[32,128,128]{2,1,0:T(8,128)(2,1)} %bitcast.8, bf16[32,6,128,128]{3,2,1,0:T(8,128)(2,1)} %adj.3), custom_call_target="tpu_custom_call" | custom-call | flops 805306368 | bytes 30000000 | tf_op jit(solution)/shard_map/spread/pallas_call | solution.py:57
  66.5 30.8 %last_exchange.1 = (bf16[8,2,128,128]{3,2,1,0:T(8,128)(2,1)}, bf16[4,1024,128]{2,1,0:T(8,128)(2,1)}, f32[8,16,512]{2,1,0:T(8,128)}) custom-call(bf16[8,2,128,128]{3,2,1,0:T(8,128)(2,1)} %bitcast.14, bf16[4,1024,128]{2,1,0:T(8,128)(2,1)} %get-tuple-element.21.out_rows, bf16[4,128,512]{2,1,0:T(8,128)(2,1)} %get-tuple-element.22.wgrad), custom_call_target="tpu_custom_call" | custom-call | tf_op jit(solution)/shard_map/last_exchange/pallas_call | solution.py:390
  97.3 0.0 copy-start
  97.3 4.4 %combine.1 = bf16[32,128,128]{2,1,0:T(8,128)(2,1)} custom-call(s32[1,8,2]{2,1,0:T(8,128)} %copy.10.send, s32[32]{0:T(128)} %occ.5, f32[32,128,128]{2,1,0:T(8,128)} %get-tuple-element.25.local, bf16[8,2,128,128]{3,2,1,0:T(8,128)(2,1)} %get-tuple-element.26.returned, f32[32,128,128]{2,1,0:T(8,128)} %get-tuple-element.17.scale_h.scale), custom_call_target="tpu_custom_call" | custom-call | tf_op jit(solution)/shard_map/combine/pallas_call | solution.py:430
  101.7 0.0 copy-start.1
  101.7 0.0 copy-done
  101.7 1.0 copy.16
  102.7 0.1 copy-done.1
  102.8 0.7 copy.17
Async XLA Ops:
  97.3 4.4 %copy-start = (bf16[4,1024,128]{2,1,0:T(8,128)(2,1)S(1)}, bf16[4,1024,128]{2,1,0:T(8,128)(2,1)}, u32[]{:S(2)}) copy-start(bf16[4,1024,128]{2,1,0:T(8,128)(2,1)} %get-tuple-element.23) | copy-start | bytes 3145732
  101.7 1.1 %copy-start.1 = (f32[8,16,512]{2,1,0:T(8,128)S(1)}, f32[8,16,512]{2,1,0:T(8,128)}, u32[]{:S(2)}) copy-start(f32[8,16,512]{2,1,0:T(8,128)} %get-tuple-element.24) | copy-start | bytes 786436

commit v4 on v3

--- a/solution.py
+++ b/solution.py
@@ -200,9 +200,9 @@
 
 def core_body(groups, neigh, occ, scaled_h, incoming_h, scale_h, adj_h, cot_h, weight_h, *refs):
     reps, rows, part = cot_h.shape
-    up, out_all, wgrad = refs[:3]
-    table, scale, adj, cot, weight, agg, agg_in, slope_all, back_all = refs[3:12]
-    loads, adj_loads, send1, recv1, send2, recv2 = refs[12:]
+    up, out_all, grads = refs[:3]
+    table, scale, adj, cot, weight, agg, agg_in, slope_all, back_all, wgrad = refs[3:13]
+    loads, adj_loads, send1, recv1, send2, recv2, send3, recv3 = refs[13:]
     me = lax.axis_index("rep")
     cells, blocks, slots, _ = adj.shape
     per_rep = cells // reps
@@ -299,6 +299,7 @@
             agg_in[q], slope_all[...], (((0,), (0,)), ((), ())), preferred_element_type=F32
         )
         wgrad[q] = term.astype(BF16)
+    backward += start_all(exchange_copies("rep", wgrad, grads, send3, recv3))
     wait_all(backward)
 
 
@@ -327,36 +328,46 @@
             VMEM(cot.shape, BF16),
             VMEM((rows, width), BF16),
             VMEM(cot.shape, BF16),
+            VMEM((reps, part, width), BF16),
             dma(5),
             dma(groups, reps),
             dma(groups, reps),
             dma(groups, reps),
             dma(groups, reps),
             dma(groups, reps),
+            dma(reps),
+            dma(reps),
         ],
         compiler_params=params(collective_id=collective_id, has_side_effects=True),
         name="core",
     )(neigh, occupancy, scaled, incoming, scale, adjacency, cot, weight)
 
 
-def last_body(factor, cut, terms, out_rows, wgrad, returned, out, grad, ph1, *sems):
+def last_body(factor, cut, terms, out_rows, grads, returned, out, grad, *sems):
     greet(("rep", "rows"))
     peers = lax.axis_size("rows")
     me = lax.axis_index("rows")
-    first = start_all(exchange_copies("rep", wgrad, ph1, sems[0], sems[1]))
-    others = start_all(exchange_copies("rows", terms, returned, sems[2], sems[3]))
-    wait_all(first)
-    others += start_all(exchange_copies("rep", out_rows, out, sems[4], sems[5]))
-    total = ph1[0].astype(F32)
-    for q in range(1, ph1.shape[0]):
-        total += ph1[q].astype(F32)
+    total = grads[0].astype(F32)
+    for q in range(1, grads.shape[0]):
+        total += grads[q].astype(F32)
+    sums = []
+    if cut:
+        held, parts = sems[4], sems[5]
+        held[...] = total.astype(BF16).reshape(held.shape)
+        sums = start_all(exchange_copies("rows", held, parts, sems[6], sems[7]))
+    mine = exchange_copies("rep", out_rows, out, sems[2], sems[3])
+    others = []
+    every = peers // len(mine)
+    for i, copy in enumerate(exchange_copies("rows", terms, returned, sems[0], sems[1])):
+        others.append(copy)
+        if i % every == 0 and mine:
+            others.append(mine.pop(0))
+    others = start_all(others + mine)
     if not cut:
         grad[...] = total
         wait_all(others)
         return
-    held, parts = sems[6], sems[7]
-    held[...] = total.astype(BF16).reshape(held.shape)
-    wait_all(start_all(exchange_copies("rows", held, parts, sems[8], sems[9])))
+    wait_all(sums)
     total = parts[0].astype(F32)
     for p in range(1, peers):
         total += parts[p].astype(F32)
@@ -367,8 +378,8 @@
             pltpu.make_async_remote_copy(
                 src_ref=grad.at[me],
                 dst_ref=grad.at[me],
-                send_sem=sems[10].at[d],
-                recv_sem=sems[11].at[d],
+                send_sem=sems[8].at[d],
+                recv_sem=sems[9].at[d],
                 device_id={"rows": lax.rem(me + d, peers)},
                 device_id_type=MESH,
             )
@@ -381,7 +392,7 @@
     peers = lax.axis_size("rows")
     reps, part, width = wgrad.shape
     cut = part % (16 * peers) == 0
-    scratch = [VMEM(wgrad.shape, BF16)] + [dma(reps)] * 2 + [dma(peers)] * 2 + [dma(reps)] * 2
+    scratch = [dma(peers)] * 2 + [dma(reps)] * 2
     grad_shape = (part, width)
     if cut:
         grad_shape = (peers, part // peers, width)

time: 104 us -> 107 us (1.029)
  Pallas kernels: 98.3 us -> 100 us
    pallas_call x1, Pallas kernels: 29.8 us -> 34.7 us  [core(): pl.pallas_call(functools.partial(core_body, groups), in_specs=[pl.BlockSp...]
    pallas_call x1, Pallas kernels: 30.8 us -> 28.1 us  [last_exchange(): pl.pallas_call(functools.partial(last_body, factor, cut), in_specs=[vmem]...]
where the time goes in v4:
time: 107 us; the launch traced here: 106 us
  Pallas kernels  100 us (93%)
  local copies, waits for them, and re-layouts  4.51 us (4%)
    pallas_call x1, Pallas kernels, core(): pl.pallas_call(functools.partial(core_body, groups), in_specs=[pl.BlockSp...  34.7 us
    pallas_call x1, Pallas kernels, last_exchange(): pl.pallas_call(functools.partial(last_body, factor, cut), in_specs=[vmem]...  28.1 us
    pallas_call x1, Pallas kernels, prepare(): pl.pallas_call(functools.partial(prepare_body, n), grid=(cells // n,), in...  24.1 us
    pallas_call x1, Pallas kernels, spread(): pl.pallas_call(functools.partial(spread_body, n), grid=(cells // n,), in_...  9.19 us
    unnamed x8, local copies, waits for them, and re-layouts  4.51 us
    pallas_call x1, Pallas kernels, combine(): pl.pallas_call(combine_body, in_specs=[pl.BlockSpec(memory_space=SMEM)] *...  4.43 us

profile of v4, /device:TPU:0, one launch (start us, length us, event | category | flops | bytes accessed | tf_op | source)
XLA Modules:
  0.0 105.7 jit_solution(6859360606134865619)
XLA Ops:
  0.6 1.3 %copy.10.send = s32[1,8,2]{2,1,0:T(8,128)} copy(s32[1,8,2]{1,2,0:T(2,128)} %param.11) | data formatting | bytes 128 | tf_op args[4]
  2.0 1.4 %copy.12.neigh = s32[32,6]{1,0:T(8,128)} copy(s32[32,6]{0,1:T(8,128)} %param.9) | data formatting | bytes 1536 | tf_op args[2]
  3.3 24.1 %prepare.1 = (f32[32,128,128]{2,1,0:T(8,128)}, bf16[32,128,128]{2,1,0:T(8,128)(2,1)}, bf16[8,2,128,128]{3,2,1,0:T(8,128)(2,1)}, bf16[4,1024,128]{2,1,0:T(8,128)(2,1)}) custom-call(s32[32]{0:T(128)} %occ.5, s32[1,8,2]{2,1,0:T(8,128)} %copy.10.send, bf16[32,128,128]{2,1,0:T(8,128)(2,1)} %bitcast.11, bf16[32,6,128,128]{3,2,1,0:T(8,128)(2,1)} %adj.3, ...), custom_call_target="tpu_custom_call" | custom-call | tf_op jit(solution)/shard_map/prepare/pallas_call | solution.py:173
  27.4 34.7 %core.1 = (bf16[4,1024,128]{2,1,0:T(8,128)(2,1)}, bf16[4,1024,128]{2,1,0:T(8,128)(2,1)}, bf16[4,128,512]{2,1,0:T(8,128)(2,1)}) custom-call(s32[32,6]{1,0:T(8,128)} %copy.12.neigh, s32[32]{0:T(128)} %occ.5, bf16[32,128,128]{2,1,0:T(8,128)(2,1)} %get-tuple-element.15.scaled_h, bf16[16,128,128]{2,1,0:T(8,128)(2,1)} %bitcast.13, ...), custom_call_target="tpu_custom_call" | custom-call | tf_op jit(solution)/shard_map/core/pallas_call | solution.py:312
  62.2 9.2 %spread.1 = (f32[32,128,128]{2,1,0:T(8,128)}, bf16[16,128,128]{2,1,0:T(8,128)(2,1)}) custom-call(s32[32,6]{1,0:T(8,128)} %copy.12.neigh, bf16[32,128,128]{2,1,0:T(8,128)(2,1)} %bitcast.8, bf16[32,6,128,128]{3,2,1,0:T(8,128)(2,1)} %adj.3), custom_call_target="tpu_custom_call" | custom-call | flops 805306368 | bytes 30000000 | tf_op jit(solution)/shard_map/spread/pallas_call | solution.py:57
  71.4 28.1 %last_exchange.1 = (bf16[8,2,128,128]{3,2,1,0:T(8,128)(2,1)}, bf16[4,1024,128]{2,1,0:T(8,128)(2,1)}, f32[8,16,512]{2,1,0:T(8,128)}) custom-call(bf16[8,2,128,128]{3,2,1,0:T(8,128)(2,1)} %bitcast.14, bf16[4,1024,128]{2,1,0:T(8,128)(2,1)} %get-tuple-element.21.out_rows, bf16[4,128,512]{2,1,0:T(8,128)(2,1)} %get-tuple-element.22.grads), custom_call_target="tpu_custom_call" | custom-call | tf_op jit(solution)/shard_map/last_exchange/pallas_call | solution.py:401
  99.4 0.0 copy-start
  99.4 4.4 %combine.1 = bf16[32,128,128]{2,1,0:T(8,128)(2,1)} custom-call(s32[1,8,2]{2,1,0:T(8,128)} %copy.10.send, s32[32]{0:T(128)} %occ.5, f32[32,128,128]{2,1,0:T(8,128)} %get-tuple-element.25.local, bf16[8,2,128,128]{3,2,1,0:T(8,128)(2,1)} %get-tuple-element.26.returned, f32[32,128,128]{2,1,0:T(8,128)} %get-tuple-element.17.scale_h.scale), custom_call_target="tpu_custom_call" | custom-call | tf_op jit(solution)/shard_map/combine/pallas_call | solution.py:441
  103.9 0.0 copy-start.1
  103.9 0.0 copy-done
  103.9 1.0 copy.16
  104.8 0.1 copy-done.1
  105.0 0.7 copy.17
Async XLA Ops:
  99.4 4.4 %copy-start = (bf16[4,1024,128]{2,1,0:T(8,128)(2,1)S(1)}, bf16[4,1024,128]{2,1,0:T(8,128)(2,1)}, u32[]{:S(2)}) copy-start(bf16[4,1024,128]{2,1,0:T(8,128)(2,1)} %get-tuple-element.23) | copy-start | bytes 3145732
  103.9 1.1 %copy-start.1 = (f32[8,16,512]{2,1,0:T(8,128)S(1)}, f32[8,16,512]{2,1,0:T(8,128)}, u32[]{:S(2)}) copy-start(f32[8,16,512]{2,1,0:T(8,128)} %get-tuple-element.24) | copy-start | bytes 786436
